TPU v7x, 256 devices: a whole 4x4x8 slice. The times are simulated.
256 devices in a mesh: img: 4 (over x), gs: 64 (over y, z, core).
Axes of the slice: x: 4, y: 4, z: 8, core: 2. Of those that a mesh axis runs over, the one named last changes fastest.
Arguments:
- params: float32 [59, 262144], P(None, 'gs'), may hold values from -4 to 1
- adam_m: float32 [59, 262144], P(None, 'gs'), may hold values from -3 to 3
- adam_v: float32 [59, 262144], P(None, 'gs'), may hold values from 0.01 to 1
- cameras: float32 [16, 16], replicated, may hold values from -4.5 to 307.2
- device_camera: int32 [4, 64], P('img'), may hold values from 0 to 15
- send_index: int32 [4, 64, 64, 64], P('img', 'gs'), may hold values from 0 to 4095
- slot_rows: int32 [4, 64, 32, 256], P('img', 'gs'), may hold values from -1 to 4095, as said below
- tile_ids: int32 [4, 64, 32], P('img', 'gs'), may hold values from 0 to 255
- target: float32 [4, 64, 32, 3, 256], P('img', 'gs'), may hold values from 0 to 1
Outputs:
- new_params: float32 [59, 262144], P(None, 'gs')
- new_m: float32 [59, 262144], P(None, 'gs')
- new_v: float32 [59, 262144], P(None, 'gs')
- rendered: float32 [4, 64, 32, 3, 256], P('img', 'gs')
Inputs may be any that keep to these rules, and one draw needn't show every extreme that they name: `slot_rows`: in each tile the live slots come first; every tile has a live slot, and the first tile of every device has all 256 live.
All inputs are finite; a program needn't handle non-finite values.
Results may differ from a plain program's by a relative error of at most 0.0003.
Values sent between devices are 32-bit elements; how exact they have to be, the bound alone decides.
No kernel may reach another device: no remote copies, remote signals or barrier semaphores. Data moves between devices by JAX's collectives and lax.ppermute only.
A program may use at most 64 MiB of HBM per device.

v0:
```python
import jax
import jax.numpy as jnp
import numpy as np
from jax import lax
from jax.sharding import PartitionSpec as P

TILE = 16
IMG_TILES = 16


sh_zero = 0.28209479177387814
sh_one = 0.4886025119029199
sh_two = (
    1.0925484305920792,
    -1.0925484305920792,
    0.31539156525252005,
    -1.0925484305920792,
    0.5462742152960396,
)
sh_three = (
    -0.5900435899266435,
    2.890611442640554,
    -0.4570457994644658,
    0.3731763325901154,
    -0.4570457994644658,
    1.445305721320277,
    -0.5900435899266435,
)
learn_rates = np.array(
    [0.00016] * 3 + [0.005] * 3 + [0.001] * 4 + [0.05] + [0.0025] * 3 + [0.000125] * 45
)
bias_first = 1.0 - 0.9**10
bias_second = 1.0 - 0.999**10


def sh_basis(dir_x, dir_y, dir_z):
    square_x = dir_x * dir_x
    square_y = dir_y * dir_y
    square_z = dir_z * dir_z
    return [
        sh_zero * jnp.ones_like(dir_x),
        -sh_one * dir_y,
        sh_one * dir_z,
        -sh_one * dir_x,
        sh_two[0] * dir_x * dir_y,
        sh_two[1] * dir_y * dir_z,
        sh_two[2] * (2.0 * square_z - square_x - square_y),
        sh_two[3] * dir_x * dir_z,
        sh_two[4] * (square_x - square_y),
        sh_three[0] * dir_y * (3.0 * square_x - square_y),
        sh_three[1] * dir_x * dir_y * dir_z,
        sh_three[2] * dir_y * (4.0 * square_z - square_x - square_y),
        sh_three[3] * dir_z * (2.0 * square_z - 3.0 * square_x - 3.0 * square_y),
        sh_three[4] * dir_x * (4.0 * square_z - square_x - square_y),
        sh_three[5] * dir_z * (square_x - square_y),
        sh_three[6] * dir_x * (square_x - 3.0 * square_y),
    ]


def project(raw, camera):
    world = [raw[0], raw[1], raw[2]]
    scales = [jnp.exp(raw[3]), jnp.exp(raw[4]), jnp.exp(raw[5])]
    quat_sq = jnp.maximum(
        raw[6] * raw[6] + raw[7] * raw[7] + raw[8] * raw[8] + raw[9] * raw[9], 0.25
    )
    inverse = lax.rsqrt(quat_sq)
    quat_w, quat_x, quat_y, quat_z = (
        raw[6] * inverse,
        raw[7] * inverse,
        raw[8] * inverse,
        raw[9] * inverse,
    )
    rotation = [
        [
            1.0 - 2.0 * (quat_y * quat_y + quat_z * quat_z),
            2.0 * (quat_x * quat_y - quat_w * quat_z),
            2.0 * (quat_x * quat_z + quat_w * quat_y),
        ],
        [
            2.0 * (quat_x * quat_y + quat_w * quat_z),
            1.0 - 2.0 * (quat_x * quat_x + quat_z * quat_z),
            2.0 * (quat_y * quat_z - quat_w * quat_x),
        ],
        [
            2.0 * (quat_x * quat_z - quat_w * quat_y),
            2.0 * (quat_y * quat_z + quat_w * quat_x),
            1.0 - 2.0 * (quat_x * quat_x + quat_y * quat_y),
        ],
    ]
    spread = [
        [rotation[first][second] * scales[second] for second in range(3)] for first in range(3)
    ]
    turn = [[camera[3 * first + second] for second in range(3)] for first in range(3)]
    viewed = [
        turn[first][0] * world[0]
        + turn[first][1] * world[1]
        + turn[first][2] * world[2]
        + camera[9 + first]
        for first in range(3)
    ]
    inv_depth = 1.0 / viewed[2]
    focal = camera[15]
    jacobian = [
        [focal * inv_depth, 0.0 * inv_depth, -focal * viewed[0] * inv_depth * inv_depth],
        [0.0 * inv_depth, focal * inv_depth, -focal * viewed[1] * inv_depth * inv_depth],
    ]
    screen = [
        [
            sum((jacobian[first][inner] * turn[inner][second] for inner in range(3)))
            for second in range(3)
        ]
        for first in range(2)
    ]
    mapped = [
        [
            sum((screen[first][inner] * spread[inner][second] for inner in range(3)))
            for second in range(3)
        ]
        for first in range(2)
    ]
    cov_xx = sum((mapped[0][inner] * mapped[0][inner] for inner in range(3))) + 0.3
    cov_xy = sum((mapped[0][inner] * mapped[1][inner] for inner in range(3)))
    cov_yy = sum((mapped[1][inner] * mapped[1][inner] for inner in range(3))) + 0.3
    determinant = cov_xx * cov_yy - cov_xy * cov_xy
    half_width = 0.5 * IMG_TILES * TILE
    ray = [world[first] - camera[12 + first] for first in range(3)]
    ray_scale = lax.rsqrt(ray[0] * ray[0] + ray[1] * ray[1] + ray[2] * ray[2])
    basis = sh_basis(ray[0] * ray_scale, ray[1] * ray_scale, ray[2] * ray_scale)
    colours = [
        jnp.maximum(
            sum((basis[term] * raw[11 + 3 * term + channel] for term in range(16))) + 0.5, 0.0
        )
        for channel in range(3)
    ]
    return jnp.stack(
        [
            focal * viewed[0] * inv_depth + half_width,
            focal * viewed[1] * inv_depth + half_width,
            cov_yy / determinant,
            -cov_xy / determinant,
            cov_xx / determinant,
            0.99 * jax.nn.sigmoid(raw[10]),
            colours[0],
            colours[1],
            colours[2],
        ]
    )


def blend(features, live, pix_x, pix_y):
    slots = live.shape[-1]
    offset_x = pix_x[:, :, None] - features[0][:, None, :]
    offset_y = pix_y[:, :, None] - features[1][:, None, :]
    power = -0.5 * (
        features[2][:, None, :] * offset_x * offset_x
        + 2.0 * features[3][:, None, :] * offset_x * offset_y
        + features[4][:, None, :] * offset_y * offset_y
    )
    alpha = features[5][:, None, :] * jnp.exp(power) * live[:, None, :]
    log_keep = jnp.log1p(-alpha)
    earlier = jnp.where(
        lax.broadcasted_iota(jnp.int32, (slots, slots), 0)
        < lax.broadcasted_iota(jnp.int32, (slots, slots), 1),
        1.0,
        0.0,
    ).astype(jnp.float32)
    passed = jnp.exp(jnp.einsum("bps,sk->bpk", log_keep, earlier, precision=lax.Precision.HIGHEST))
    weight = passed * alpha
    return jnp.einsum("bps,cbs->bcp", weight, features[6:9], precision=lax.Precision.HIGHEST)


def render_tiles(features, slot_rows, tile_ids, target):
    tiles, slots = slot_rows.shape
    width = features.shape[0]
    live = slot_rows >= 0
    safe = jnp.where(live, slot_rows, 0)
    live_float = jnp.where(live, 1.0, 0.0).astype(jnp.float32)
    gathered = jnp.take(features, safe.reshape(-1), axis=1).reshape(width, tiles, slots)
    lane = lax.iota(jnp.int32, TILE * TILE)
    pix_x = (tile_ids[:, None] % IMG_TILES * TILE + lane[None, :] % TILE).astype(jnp.float32) + 0.5
    pix_y = (tile_ids[:, None] // IMG_TILES * TILE + lane[None, :] // TILE).astype(
        jnp.float32
    ) + 0.5
    groups = tiles // 4
    stacked = (
        gathered.reshape(width, groups, 4, slots).transpose(1, 0, 2, 3),
        live_float.reshape(groups, 4, slots),
        pix_x.reshape(groups, 4, -1),
        pix_y.reshape(groups, 4, -1),
        target.reshape(groups, 4, 3, -1),
    )

    def shade(block):
        feats_block, live_block, across, down, wanted = block
        colour, pull = jax.vjp(
            lambda part_feats: blend(part_feats, live_block, across, down), feats_block
        )
        (slot_grad,) = pull(colour - wanted)
        return (colour, slot_grad)

    colours, grads = lax.map(shade, stacked)
    slot_grads = grads.transpose(1, 0, 2, 3).reshape(width, tiles * slots)
    row_grads = jax.ops.segment_sum(
        slot_grads.T, safe.reshape(-1), num_segments=features.shape[1]
    ).T
    return (colours.reshape(tiles, 3, -1), row_grads)


def adam_update(params, adam_m, adam_v, gradient):
    rates = jnp.asarray(learn_rates, jnp.float32)[:, None]
    new_m = 0.9 * adam_m + 0.1 * gradient
    new_v = 0.999 * adam_v + 0.001 * gradient * gradient
    new_params = params - rates * (new_m / bias_first) / (jnp.sqrt(new_v / bias_second) + 1e-08)
    return (new_params, new_m, new_v)


def on_device(
    params, adam_m, adam_v, cameras, device_camera, send_index, slot_rows, tile_ids, target
):
    n_gs = lax.axis_size("gs")
    capacity = send_index.shape[-1]
    width = params.shape[0]
    local = send_index[0, 0].reshape(-1)
    outgoing = jnp.take(params, local, axis=1)
    dest_cameras = jnp.take(cameras, device_camera[0], axis=1)
    own_camera = jnp.take(dest_cameras, lax.axis_index("gs")[None], axis=1)
    incoming = lax.all_to_all(
        outgoing.reshape(width, n_gs, capacity), "gs", split_axis=1, concat_axis=1, tiled=True
    ).reshape(width, -1)
    features, pull = jax.vjp(lambda raw: project(raw, own_camera), incoming)
    colours, row_grads = render_tiles(features, slot_rows[0, 0], tile_ids[0, 0], target[0, 0])
    (raw_grads,) = pull(row_grads)
    sent_grads = lax.all_to_all(
        raw_grads.reshape(width, n_gs, capacity), "gs", split_axis=1, concat_axis=1, tiled=True
    ).reshape(width, -1)
    gradient = jax.ops.segment_sum(sent_grads.T, local, num_segments=params.shape[1]).T
    total = lax.psum(gradient, "img")
    new_params, new_m, new_v = adam_update(params, adam_m, adam_v, total)
    return (new_params, new_m, new_v, colours[None, None])


def solution(mesh):
    return jax.shard_map(
        on_device,
        mesh=mesh,
        in_specs=(
            P(None, "gs"),
            P(None, "gs"),
            P(None, "gs"),
            P(),
            P("img", None),
            P("img", "gs", None, None),
            P("img", "gs", None, None),
            P("img", "gs", None),
            P("img", "gs", None, None, None),
        ),
        out_specs=(P(None, "gs"), P(None, "gs"), P(None, "gs"), P("img", "gs", None, None, None)),
        check_vma=False,
    )
```

profile of v0, /device:TPU:8, one launch (start us, length us, event | category | flops | bytes accessed | tf_op | source)
XLA Modules:
  0.0 478.4 jit_solution(9635254371683510222)
XLA Ops:
  8.8 1.9 copy.105
  10.7 14.1 %gather_fusion.1 = f32[4096,59]{1,0:T(8,128)} fusion(f32[59,4096]{0,1:T(8,128)S(1)} %copy.105, s32[4096]{0:T(1024)S(1)} %broadcast_clamp_fusion.1), kind=kCustom, calls=%fused_computation.1 | custom fusion | bytes 1949696 | tf_op jit(solution)/shard_map/jit(_take)/gather | solution.py:224
  24.8 2.1 copy.106
  26.9 1.6 fusion.134
  28.5 3.6 reshape.5819
  32.1 12.3 %all-to-all-start = ((f32[64,1,3776]{2,1,0:T(1,128)}), f32[64,1,3776]{2,1,0:T(1,128)S(1)}, u32[]{:S(2)}, u32[]{:S(2)}) async-start(f32[64,1,3776]{2,1,0:T(1,128)} %reshape.5819), calls=%async_computation | async-start | bytes 1966080 | tf_op jit(solution)/shard_map/all_to_all | solution.py:227
  56.0 14.0 %all-to-all-done = f32[64,1,3776]{2,1,0:T(1,128)S(1)} async-done(((f32[64,1,3776]{2,1,0:T(1,128)}), f32[64,1,3776]{2,1,0:T(1,128)S(1)}, u32[]{:S(2)}, u32[]{:S(2)}) %all-to-all-start) | async-done | bytes 966688 | tf_op jit(solution)/shard_map/all_to_all | solution.py:227
  70.5 3.0 reduce.224
  74.5 2.2 slice_reduce_fusion.14
  76.7 2.2 slice_reduce_fusion.2
  79.0 2.4 slice_reduce_fusion.1
  81.4 10.0 %broadcast_multiply_fusion.2 = (f32[1,64,64]{2,1,0:T(8,128)S(1)}, f32[1,64,64]{2,1,0:T(8,128)S(1)}, f32[1,64,64]{2,1,0:T(8,128)}, f32[1,64,64]{2,1,0:T(8,128)S(1...) fusion(f32[]{:T(128)} %bitcast.33, f32[]{:T(128)} %bitcast.32, ...), kind=kLoop, calls=%fused_computation.230 | loop fusion | flops 102400 | bytes 196672 | tf_op jit(solution)/shard_map/jvp()/mul | solution.py:105
  110.3 8.1 %fusion.127 = (f32[1,4096]{1,0:T(1,128)S(1)}, f32[1,4096]{1,0:T(1,128)S(1)}, f32[1,4096]{1,0:T(1,128)}, f32[1,4096]{1,0:T(1,128)S(1)}, f32[1,4096]{1,0:T(1,128)}...) fusion(f32[]{:T(128)} %bitcast.25, ...), kind=kLoop, calls=%fused_computation.420 | loop fusion | flops 561152 | bytes 802880 | tf_op jit(solution)/shard_map/jvp()/div | solution.py:141
  122.1 30.4 %gather_fusion.2 = f32[8192,9]{1,0:T(8,128)} fusion(f32[9,4096]{0,1:T(8,128)S(1)} %copy.111, s32[8192]{0:T(1024)} %broadcast_clamp_fusion), kind=kCustom, calls=%fused_computation.2 | custom fusion | bytes 622592 | tf_op jit(solution)/shard_map/jit(_take)/gather | solution.py:178
  152.5 2.9 copy.112
  155.5 106.3 %while.13 = (s32[]{:T(128)}, f32[8,4,3,256]{3,2,1,0:T(4,128)}, f32[8,9,4,256]{3,1,2,0:T(8,128)S(1)}, f32[8,9,4,256]{3,1,2,0:T(8,128)S(1)}, f32[8,4,256]{2,1,0:T(...) while((s32[]{:T(128)}, f32[8,4,3,256]{3,2,1,0:T(4,128)}, ...), condition=%wide.region_7.8_spmd, body=%wide.region_0.7_spmd.sunk | while | flops 1665984512 | bytes 11102505 | solution.py:201
  157.0 2.7 convolution_exponential_fusion.2
  159.7 3.4 bitcast_dynamic-update-slice_fusion.4
  163.2 1.2 convolution_bitcast_fusion.2
  165.5 3.2 fusion.144
  170.3 2.7 convolution_exponential_fusion.2
  173.0 3.4 bitcast_dynamic-update-slice_fusion.4
  176.5 1.2 convolution_bitcast_fusion.2
  178.7 3.2 fusion.144
  183.5 2.7 convolution_exponential_fusion.2
  186.3 3.4 bitcast_dynamic-update-slice_fusion.4
  189.7 1.2 convolution_bitcast_fusion.2
  192.0 3.2 fusion.144
  196.8 2.7 convolution_exponential_fusion.2
  199.6 3.4 bitcast_dynamic-update-slice_fusion.4
  203.0 1.2 convolution_bitcast_fusion.2
  205.3 3.2 fusion.144
  210.1 2.7 convolution_exponential_fusion.2
  212.9 3.4 bitcast_dynamic-update-slice_fusion.4
  218.6 3.2 fusion.144
  223.4 2.7 convolution_exponential_fusion.2
  226.2 3.4 bitcast_dynamic-update-slice_fusion.4
  231.9 3.2 fusion.144
  236.7 2.7 convolution_exponential_fusion.2
  239.5 3.4 bitcast_dynamic-update-slice_fusion.4
  242.9 1.2 convolution_bitcast_fusion.2
  245.2 3.2 fusion.144
  250.0 2.7 convolution_exponential_fusion.2
  252.7 3.4 bitcast_dynamic-update-slice_fusion.4
  258.5 3.2 fusion.144
  262.2 2.6 copy.115
  264.8 55.3 %scatter_custom_fusion = f32[4096,9]{1,0:T(8,128)S(1)} fusion(s32[8192]{0:T(1024)} %bitcast.162, f32[8192,9]{1,0:T(8,128)} %copy.115, f32[]{:T(128)} %constant.105.clone.1), kind=kCustom, calls=%fused_computation.107 | custom fusion | flops 73728 | bytes 147968 | tf_op jit(solution)/shard_map/scatter-add | solution.py:203
  322.8 1.4 fusion.119
  327.7 7.6 %multiply_add_fusion.8 = (f32[1,4096]{1,0:T(1,128)S(1)}, f32[1,4096]{1,0:T(1,128)S(1)}, f32[1,4096]{1,0:T(1,128)S(1)}, f32[1,4096]{1,0:T(1,128)S(1)}, f32[1,4096...) fusion(f32[1,4096]{1,0:T(1,128)S(1)} %sub.1849, f32[]{:T(128)} %bitcast.23, f32[]{:T(128)} %bitcast.27, ...), kind=kLoop, calls=%fused_computation.245 | loop fusion | flops 1101824 | bytes 1245228 | tf_op jit(solution)/shard_map/transpose(jvp())/add_any | solution.py:97
  335.3 3.9 multiply_add_fusion.7
  339.3 3.3 fusion.58
  342.6 2.1 reshape.5401
  344.7 2.7 copy.141
  347.4 2.3 reshape.5821
  349.7 7.5 %all-to-all-start.1 = ((f32[64,1,3776]{2,1,0:T(1,128)}), f32[64,1,3776]{2,1,0:T(1,128)S(1)}, u32[]{:S(2)}, u32[]{:S(2)}) async-start(f32[64,1,3776]{2,1,0:T(1,128)} %reshape.5821), calls=%async_computation.1 | async-start | bytes 1966080 | tf_op jit(solution)/shard_map/all_to_all | solution.py:233
  357.5 25.4 %all-to-all-done.1 = f32[64,1,3776]{2,1,0:T(1,128)S(1)} async-done(((f32[64,1,3776]{2,1,0:T(1,128)}), f32[64,1,3776]{2,1,0:T(1,128)S(1)}, u32[]{:S(2)}, u32[]{:S(2)}) %all-to-all-start.1) | async-done | bytes 966688 | tf_op jit(solution)/shard_map/all_to_all | solution.py:233
  383.0 3.0 reduce.225
  386.8 2.4 copy.118
  389.2 2.1 reshape.5402
  391.3 2.0 copy.119
  393.3 23.2 %scatter_custom_fusion.1 = f32[4096,59]{1,0:T(8,128)S(1)} fusion(s32[4096]{0:T(1024)S(1)} %reshape.5516, f32[4096,59]{1,0:T(8,128)} %copy.119, f32[]{:T(128)} %constant.105.clone.1), kind=kCustom, calls=%fused_computation.109 | custom fusion | flops 241664 | bytes 967168 | tf_op jit(solution)/shard_map/scatter-add | solution.py:236
  416.5 1.6 copy.120
  418.8 48.6 %all-reduce.72.cloned.1.call-done = f32[59,4096]{1,0:T(8,128)} async-done(((f32[59,4096]{1,0:T(8,128)}), f32[59,4096]{1,0:T(8,128)}) %all-reduce.72.cloned.1.call-update) | async-done | bytes 966672 | tf_op jit(solution)/shard_map/psum | solution.py:237
  467.4 3.9 divide_subtract_fusion
  (424 shorter events, 64.7 us)
Async XLA Ops:
  28.5 15.9 %copy-start.70 = (s32[1,64]{1,0:T(1,128)S(1)}, s32[1,64]{1,0:T(1,128)}, u32[]{:S(2)}) copy-start(s32[1,64]{1,0:T(1,128)} %param.16) | copy-start | bytes 772
  28.5 16.0 %copy-start.50 = (s32[1,1,32,256]{3,2,1,0:T(8,128)S(1)}, s32[1,1,32,256]{3,2,1,0:T(8,128)}, u32[]{:S(2)}) copy-start(s32[1,1,32,256]{3,2,1,0:T(8,128)} %param.18) | copy-start | bytes 98308
  28.5 17.3 %copy-start.68 = (f32[16,16]{1,0:T(8,128)S(1)}, f32[16,16]{1,0:T(8,128)}, u32[]{:S(2)}) copy-start(f32[16,16]{1,0:T(8,128)} %param.15) | copy-start | bytes 3076
  28.5 24.6 %copy-start.71 = (s32[1,1,32]{2,1,0:T(1,128)S(1)}, s32[1,1,32]{2,1,0:T(1,128)}, u32[]{:S(2)}) copy-start(s32[1,1,32]{2,1,0:T(1,128)} %param.19) | copy-start | bytes 388
  28.5 25.4 %copy-start.51 = (f32[1,1,32,3,256]{4,2,3,1,0:T(8,128)S(1)}, f32[1,1,32,3,256]{4,2,3,1,0:T(8,128)}, u32[]{:S(2)}) copy-start(f32[1,1,32,3,256]{4,2,3,1,0:T(8,128)} %param.20) | copy-start | bytes 294916
  32.1 37.9 %all-to-all-start = ((f32[64,1,3776]{2,1,0:T(1,128)}), f32[64,1,3776]{2,1,0:T(1,128)S(1)}, u32[]{:S(2)}, u32[]{:S(2)}) async-start(f32[64,1,3776]{2,1,0:T(1,128)} %reshape.5819), calls=%async_computation | async-start | bytes 1966080 | tf_op jit(solution)/shard_map/all_to_all | solution.py:227
  81.3 24.6 %copy-start.49 = (f32[64,64]{1,0:T(8,128)S(1)}, f32[64,64]{1,0:T(8,128)}, u32[]{:S(2)}) copy-start(f32[64,64]{1,0:T(8,128)} %get-tuple-element.127) | copy-start | bytes 49156
  81.3 24.7 %copy-start.48 = (f32[64,64]{1,0:T(8,128)S(1)}, f32[64,64]{1,0:T(8,128)}, u32[]{:S(2)}) copy-start(f32[64,64]{1,0:T(8,128)} %get-tuple-element.126) | copy-start | bytes 49156
  81.3 24.8 %copy-start.47 = (f32[64,64]{1,0:T(8,128)S(1)}, f32[64,64]{1,0:T(8,128)}, u32[]{:S(2)}) copy-start(f32[64,64]{1,0:T(8,128)} %get-tuple-element.125) | copy-start | bytes 49156
  81.3 24.9 %copy-start.46 = (f32[64,64]{1,0:T(8,128)S(1)}, f32[64,64]{1,0:T(8,128)}, u32[]{:S(2)}) copy-start(f32[64,64]{1,0:T(8,128)} %get-tuple-element.124) | copy-start | bytes 49156
  81.3 25.0 %copy-start.45 = (f32[64,64]{1,0:T(8,128)S(1)}, f32[64,64]{1,0:T(8,128)}, u32[]{:S(2)}) copy-start(f32[64,64]{1,0:T(8,128)} %get-tuple-element.123) | copy-start | bytes 49156
  81.3 25.1 %copy-start.44 = (f32[64,64]{1,0:T(8,128)S(1)}, f32[64,64]{1,0:T(8,128)}, u32[]{:S(2)}) copy-start(f32[64,64]{1,0:T(8,128)} %get-tuple-element.122) | copy-start | bytes 49156
  81.3 25.2 %copy-start.43 = (f32[64,64]{1,0:T(8,128)S(1)}, f32[64,64]{1,0:T(8,128)}, u32[]{:S(2)}) copy-start(f32[64,64]{1,0:T(8,128)} %get-tuple-element.121) | copy-start | bytes 49156
  81.4 25.3 %copy-start.42 = (f32[64,64]{1,0:T(8,128)S(1)}, f32[64,64]{1,0:T(8,128)}, u32[]{:S(2)}) copy-start(f32[64,64]{1,0:T(8,128)} %get-tuple-element.120) | copy-start | bytes 49156
  81.4 25.4 %copy-start.41 = (f32[64,64]{1,0:T(8,128)S(1)}, f32[64,64]{1,0:T(8,128)}, u32[]{:S(2)}) copy-start(f32[64,64]{1,0:T(8,128)} %get-tuple-element.119) | copy-start | bytes 49156
  99.2 20.4 %copy-start.27 = (f32[1,4096]{1,0:T(1,128)}, f32[1,4096]{1,0:T(1,128)S(1)}, u32[]{:S(2)}) copy-start(f32[1,4096]{1,0:T(1,128)S(1)} %squeeze.259) | copy-start | bytes 49156
  105.8 15.3 %copy-start.31 = (f32[1,4096]{1,0:T(1,128)}, f32[1,4096]{1,0:T(1,128)S(1)}, u32[]{:S(2)}) copy-start(f32[1,4096]{1,0:T(1,128)S(1)} %squeeze.244) | copy-start | bytes 49156
  106.5 14.6 %copy-start.3 = (f32[1,4096]{1,0:T(1,128)}, f32[1,4096]{1,0:T(1,128)S(1)}, u32[]{:S(2)}) copy-start(f32[1,4096]{1,0:T(1,128)S(1)} %squeeze.220) | copy-start | bytes 49156
  106.6 14.5 %copy-start.5 = (f32[1,4096]{1,0:T(1,128)}, f32[1,4096]{1,0:T(1,128)S(1)}, u32[]{:S(2)}) copy-start(f32[1,4096]{1,0:T(1,128)S(1)} %squeeze.221) | copy-start | bytes 49156
  106.8 14.4 %copy-start.7 = (f32[1,4096]{1,0:T(1,128)}, f32[1,4096]{1,0:T(1,128)S(1)}, u32[]{:S(2)}) copy-start(f32[1,4096]{1,0:T(1,128)S(1)} %squeeze.222) | copy-start | bytes 49156
  106.9 14.3 %copy-start.9 = (f32[1,4096]{1,0:T(1,128)}, f32[1,4096]{1,0:T(1,128)S(1)}, u32[]{:S(2)}) copy-start(f32[1,4096]{1,0:T(1,128)S(1)} %squeeze.223) | copy-start | bytes 49156
  107.0 14.2 %copy-start.11 = (f32[1,4096]{1,0:T(1,128)}, f32[1,4096]{1,0:T(1,128)S(1)}, u32[]{:S(2)}) copy-start(f32[1,4096]{1,0:T(1,128)S(1)} %squeeze.224) | copy-start | bytes 49156
  107.1 14.1 %copy-start.13 = (f32[1,4096]{1,0:T(1,128)}, f32[1,4096]{1,0:T(1,128)S(1)}, u32[]{:S(2)}) copy-start(f32[1,4096]{1,0:T(1,128)S(1)} %squeeze.225) | copy-start | bytes 49156
  107.2 14.0 %copy-start.15 = (f32[1,4096]{1,0:T(1,128)}, f32[1,4096]{1,0:T(1,128)S(1)}, u32[]{:S(2)}) copy-start(f32[1,4096]{1,0:T(1,128)S(1)} %squeeze.226) | copy-start | bytes 49156
  107.3 14.0 %copy-start.17 = (f32[1,4096]{1,0:T(1,128)}, f32[1,4096]{1,0:T(1,128)S(1)}, u32[]{:S(2)}) copy-start(f32[1,4096]{1,0:T(1,128)S(1)} %squeeze.227) | copy-start | bytes 49156
  107.4 13.9 %copy-start.19 = (f32[1,4096]{1,0:T(1,128)}, f32[1,4096]{1,0:T(1,128)S(1)}, u32[]{:S(2)}) copy-start(f32[1,4096]{1,0:T(1,128)S(1)} %squeeze.228) | copy-start | bytes 49156
  107.5 13.8 %copy-start.34 = (f32[1,4096]{1,0:T(1,128)}, f32[1,4096]{1,0:T(1,128)S(1)}, u32[]{:S(2)}) copy-start(f32[1,4096]{1,0:T(1,128)S(1)} %squeeze.229) | copy-start | bytes 49156
  108.5 9.9 %copy-start.21 = (f32[1,4096]{1,0:T(1,128)}, f32[1,4096]{1,0:T(1,128)S(1)}, u32[]{:S(2)}) copy-start(f32[1,4096]{1,0:T(1,128)S(1)} %reshape.5434) | copy-start | bytes 49156
  108.6 9.8 %copy-start.23 = (f32[1,4096]{1,0:T(1,128)}, f32[1,4096]{1,0:T(1,128)S(1)}, u32[]{:S(2)}) copy-start(f32[1,4096]{1,0:T(1,128)S(1)} %reshape.5436) | copy-start | bytes 49156
  109.2 9.2 %copy-start.37 = (f32[1,4096]{1,0:T(1,128)}, f32[1,4096]{1,0:T(1,128)S(1)}, u32[]{:S(2)}) copy-start(f32[1,4096]{1,0:T(1,128)S(1)} %squeeze.214) | copy-start | bytes 49156
  110.1 8.3 %copy-start.29 = (f32[1,4096]{1,0:T(1,128)}, f32[1,4096]{1,0:T(1,128)S(1)}, u32[]{:S(2)}) copy-start(f32[1,4096]{1,0:T(1,128)S(1)} %reshape.5428) | copy-start | bytes 49156
  110.2 8.2 %copy-start.36 = (f32[1,4096]{1,0:T(1,128)}, f32[1,4096]{1,0:T(1,128)S(1)}, u32[]{:S(2)}) copy-start(f32[1,4096]{1,0:T(1,128)S(1)} %div.302) | copy-start | bytes 49156
  320.7 6.5 %copy-start.58 = (f32[1,4096]{1,0:T(1,128)S(1)}, f32[1,4096]{1,0:T(1,128)}, u32[]{:S(2)}) copy-start(f32[1,4096]{1,0:T(1,128)} %get-tuple-element.237) | copy-start | bytes 49156
  320.7 6.5 %copy-start.59 = (f32[1,4096]{1,0:T(1,128)S(1)}, f32[1,4096]{1,0:T(1,128)}, u32[]{:S(2)}) copy-start(f32[1,4096]{1,0:T(1,128)} %get-tuple-element.238) | copy-start | bytes 49156
  320.8 6.5 %copy-start.60 = (f32[1,4096]{1,0:T(1,128)S(1)}, f32[1,4096]{1,0:T(1,128)}, u32[]{:S(2)}) copy-start(f32[1,4096]{1,0:T(1,128)} %get-tuple-element.240) | copy-start | bytes 49156
  320.8 6.5 %copy-start.61 = (f32[1,4096]{1,0:T(1,128)S(1)}, f32[1,4096]{1,0:T(1,128)}, u32[]{:S(2)}) copy-start(f32[1,4096]{1,0:T(1,128)} %get-tuple-element.243) | copy-start | bytes 49156
  320.8 6.5 %copy-start.62 = (f32[1,4096]{1,0:T(1,128)S(1)}, f32[1,4096]{1,0:T(1,128)}, u32[]{:S(2)}) copy-start(f32[1,4096]{1,0:T(1,128)} %get-tuple-element.245) | copy-start | bytes 49156
  320.8 6.5 %copy-start.63 = (f32[1,4096]{1,0:T(1,128)S(1)}, f32[1,4096]{1,0:T(1,128)}, u32[]{:S(2)}) copy-start(f32[1,4096]{1,0:T(1,128)} %get-tuple-element.246) | copy-start | bytes 49156
  320.8 6.5 %copy-start.64 = (f32[1,4096]{1,0:T(1,128)S(1)}, f32[1,4096]{1,0:T(1,128)}, u32[]{:S(2)}) copy-start(f32[1,4096]{1,0:T(1,128)} %get-tuple-element.249) | copy-start | bytes 49156
  320.8 6.7 %copy-start.4 = (f32[1,4096]{1,0:T(1,128)S(1)}, f32[1,4096]{1,0:T(1,128)}, u32[]{:S(2)}) copy-start(f32[1,4096]{1,0:T(1,128)} %copy-done.3) | copy-start | bytes 49156
  320.8 6.7 %copy-start.6 = (f32[1,4096]{1,0:T(1,128)S(1)}, f32[1,4096]{1,0:T(1,128)}, u32[]{:S(2)}) copy-start(f32[1,4096]{1,0:T(1,128)} %copy-done.5) | copy-start | bytes 49156
  320.8 6.7 %copy-start.8 = (f32[1,4096]{1,0:T(1,128)S(1)}, f32[1,4096]{1,0:T(1,128)}, u32[]{:S(2)}) copy-start(f32[1,4096]{1,0:T(1,128)} %copy-done.7) | copy-start | bytes 49156
  320.9 6.7 %copy-start.10 = (f32[1,4096]{1,0:T(1,128)S(1)}, f32[1,4096]{1,0:T(1,128)}, u32[]{:S(2)}) copy-start(f32[1,4096]{1,0:T(1,128)} %copy-done.9) | copy-start | bytes 49156
  320.9 6.7 %copy-start.12 = (f32[1,4096]{1,0:T(1,128)S(1)}, f32[1,4096]{1,0:T(1,128)}, u32[]{:S(2)}) copy-start(f32[1,4096]{1,0:T(1,128)} %copy-done.11) | copy-start | bytes 49156
  320.9 6.7 %copy-start.14 = (f32[1,4096]{1,0:T(1,128)S(1)}, f32[1,4096]{1,0:T(1,128)}, u32[]{:S(2)}) copy-start(f32[1,4096]{1,0:T(1,128)} %copy-done.13) | copy-start | bytes 49156
  320.9 6.7 %copy-start.16 = (f32[1,4096]{1,0:T(1,128)S(1)}, f32[1,4096]{1,0:T(1,128)}, u32[]{:S(2)}) copy-start(f32[1,4096]{1,0:T(1,128)} %copy-done.15) | copy-start | bytes 49156
  320.9 6.7 %copy-start.18 = (f32[1,4096]{1,0:T(1,128)S(1)}, f32[1,4096]{1,0:T(1,128)}, u32[]{:S(2)}) copy-start(f32[1,4096]{1,0:T(1,128)} %copy-done.17) | copy-start | bytes 49156
  320.9 6.7 %copy-start.20 = (f32[1,4096]{1,0:T(1,128)S(1)}, f32[1,4096]{1,0:T(1,128)}, u32[]{:S(2)}) copy-start(f32[1,4096]{1,0:T(1,128)} %copy-done.19) | copy-start | bytes 49156
  320.9 6.7 %copy-start.22 = (f32[1,4096]{1,0:T(1,128)S(1)}, f32[1,4096]{1,0:T(1,128)}, u32[]{:S(2)}) copy-start(f32[1,4096]{1,0:T(1,128)} %copy-done.21) | copy-start | bytes 49156
  320.9 6.7 %copy-start.24 = (f32[1,4096]{1,0:T(1,128)S(1)}, f32[1,4096]{1,0:T(1,128)}, u32[]{:S(2)}) copy-start(f32[1,4096]{1,0:T(1,128)} %copy-done.23) | copy-start | bytes 49156
  320.9 6.7 %copy-start.26 = (f32[1,4096]{1,0:T(1,128)S(1)}, f32[1,4096]{1,0:T(1,128)}, u32[]{:S(2)}) copy-start(f32[1,4096]{1,0:T(1,128)} %copy-done.25) | copy-start | bytes 49156
  320.9 6.7 %copy-start.30 = (f32[1,4096]{1,0:T(1,128)S(1)}, f32[1,4096]{1,0:T(1,128)}, u32[]{:S(2)}) copy-start(f32[1,4096]{1,0:T(1,128)} %copy-done.29) | copy-start | bytes 49156
  321.0 6.7 %copy-start.33 = (f32[1,4096]{1,0:T(1,128)S(1)}, f32[1,4096]{1,0:T(1,128)}, u32[]{:S(2)}) copy-start(f32[1,4096]{1,0:T(1,128)} %get-tuple-element.219) | copy-start | bytes 49156
  321.0 6.7 %copy-start.52 = (f32[1,4096]{1,0:T(1,128)S(1)}, f32[1,4096]{1,0:T(1,128)}, u32[]{:S(2)}) copy-start(f32[1,4096]{1,0:T(1,128)} %get-tuple-element.234) | copy-start | bytes 49156
  321.0 6.7 %copy-start.53 = (f32[1,4096]{1,0:T(1,128)S(1)}, f32[1,4096]{1,0:T(1,128)}, u32[]{:S(2)}) copy-start(f32[1,4096]{1,0:T(1,128)} %get-tuple-element.262) | copy-start | bytes 49156
  324.2 15.0 %copy-start.54 = (f32[1,4096]{1,0:T(1,128)S(1)}, f32[1,4096]{1,0:T(1,128)}, u32[]{:S(2)}) copy-start(f32[1,4096]{1,0:T(1,128)} %get-tuple-element.239) | copy-start | bytes 49156
  324.2 15.0 %copy-start.55 = (f32[1,4096]{1,0:T(1,128)S(1)}, f32[1,4096]{1,0:T(1,128)}, u32[]{:S(2)}) copy-start(f32[1,4096]{1,0:T(1,128)} %get-tuple-element.241) | copy-start | bytes 49156
  324.2 15.0 %copy-start.56 = (f32[1,4096]{1,0:T(1,128)S(1)}, f32[1,4096]{1,0:T(1,128)}, u32[]{:S(2)}) copy-start(f32[1,4096]{1,0:T(1,128)} %get-tuple-element.250) | copy-start | bytes 49156
  324.2 15.0 %copy-start.57 = (f32[1,4096]{1,0:T(1,128)S(1)}, f32[1,4096]{1,0:T(1,128)}, u32[]{:S(2)}) copy-start(f32[1,4096]{1,0:T(1,128)} %get-tuple-element.253) | copy-start | bytes 49156
  347.3 10.1 %copy-start.2 = (s32[1,1,64,64]{3,2,1,0:T(8,128)S(1)}, s32[1,1,64,64]{3,2,1,0:T(8,128)}, u32[]{:S(2)}) copy-start(s32[1,1,64,64]{3,2,1,0:T(8,128)} %param.17) | copy-start | bytes 49156
  349.7 33.3 %all-to-all-start.1 = ((f32[64,1,3776]{2,1,0:T(1,128)}), f32[64,1,3776]{2,1,0:T(1,128)S(1)}, u32[]{:S(2)}, u32[]{:S(2)}) async-start(f32[64,1,3776]{2,1,0:T(1,128)} %reshape.5821), calls=%async_computation.1 | async-start | bytes 1966080 | tf_op jit(solution)/shard_map/all_to_all | solution.py:233
  357.2 110.2 %all-reduce.72.cloned.1.call-start = ((), (), s32[]{:S(2)}) async-start(), calls=%async_computation.2 | async-start | bytes 2097152 | tf_op jit(solution)/shard_map/psum | solution.py:237
  416.5 50.9 %copy-start = (f32[59,4096]{1,0:T(8,128)S(1)}, f32[59,4096]{1,0:T(8,128)}, u32[]{:S(2)}) copy-start(f32[59,4096]{1,0:T(8,128)} %param.12) | copy-start | bytes 2899972
  416.5 50.9 %copy-start.69 = (f32[59]{0:T(128)S(1)}, f32[59]{0:T(128)}, u32[]{:S(2)}) copy-start(f32[59]{0:T(128)} %constant.374) | copy-start | bytes 712
  (19 other events, 77.1 us)
Sparse Core Ops, SparseCore 0:
  418.3 49.1 all-reduce.71
where the time goes:
time: 485 us; the launch traced here: 478 us
  other arithmetic  146 us (30%)
  local copies, waits for them, and re-layouts  110 us (23%)
  matrix products  93 us (19%)
  waiting for transfers between devices  88.1 us (18%)
  between operations  20.1 us (4%)
  starting transfers between devices  20 us (4%)
    scatter-add x1, other arithmetic, render_tiles(): jax.ops.segment_sum(slot_grads.T, safe.reshape(-1), num_segments=features...  55.3 us
    psum x1, waiting for transfers between devices, on_device(): total = lax.psum(gradient, 'img')  48.6 us
    dot_general x16, matrix products, blend(): jnp.einsum('bps,sk->bpk', log_keep, earlier, precision=lax.Precision.HIGH...  47.2 us
    dot_general x24, matrix products, blend(): jnp.einsum('bps,cbs->bcp', weight, features[6:9], precision=lax.Precision...  45.9 us
    gather x2, local copies, waits for them, and re-layouts, render_tiles(): jnp.take(features, safe.reshape(-1), axis=1).reshape(width, tiles, slots)  33.3 us
    all_to_all x1, waiting for transfers between devices, on_device(): lax.all_to_all(raw_grads.reshape(width, n_gs, capacity), 'gs', split_axis...  25.4 us
    scatter-add x1, other arithmetic, on_device(): jax.ops.segment_sum(sent_grads.T, local, num_segments=params.shape[1])  23.2 us
    gather x2, local copies, waits for them, and re-layouts, on_device(): outgoing = jnp.take(params, local, axis=1)  16.2 us
  transfers between devices with their start and end apart: 3, of which 3 were waited for; matrix products, arithmetic and copies ran while one was open for 2% of the time, Pallas kernels for 0%

commit v1 on v0

--- a/solution.py
+++ b/solution.py
@@ -2,6 +2,8 @@
 import jax.numpy as jnp
 import numpy as np
 from jax import lax
+from jax.experimental import pallas as pl
+from jax.experimental.pallas import tpu as pltpu
 from jax.sharding import PartitionSpec as P
 
 TILE = 16
@@ -147,63 +149,254 @@
     )
 
 
-def blend(features, live, pix_x, pix_y):
-    slots = live.shape[-1]
-    offset_x = pix_x[:, :, None] - features[0][:, None, :]
-    offset_y = pix_y[:, :, None] - features[1][:, None, :]
-    power = -0.5 * (
-        features[2][:, None, :] * offset_x * offset_x
-        + 2.0 * features[3][:, None, :] * offset_x * offset_y
-        + features[4][:, None, :] * offset_y * offset_y
-    )
-    alpha = features[5][:, None, :] * jnp.exp(power) * live[:, None, :]
-    log_keep = jnp.log1p(-alpha)
-    earlier = jnp.where(
-        lax.broadcasted_iota(jnp.int32, (slots, slots), 0)
-        < lax.broadcasted_iota(jnp.int32, (slots, slots), 1),
-        1.0,
+F32, BF16, I32 = jnp.float32, jnp.bfloat16, jnp.int32
+NN = (((1,), (0,)), ((), ()))
+NT = (((1,), (1,)), ((), ()))
+LN2 = float(np.log(2.0))
+
+
+def dot(left, right, dims=NN):
+    return lax.dot_general(left, right, dims, preferred_element_type=F32)
+
+
+def split2(value):
+    high = value.astype(BF16)
+    return high, (value - high.astype(F32)).astype(BF16)
+
+
+def split3(value):
+    high = value.astype(BF16)
+    rest = value - high.astype(F32)
+    mid = rest.astype(BF16)
+    return high, mid, (rest - mid.astype(F32)).astype(BF16)
+
+
+def iota(shape, dim):
+    return lax.broadcasted_iota(I32, shape, dim)
+
+
+def render_kernel(
+    tid_ref, recv_ref, slots_ref, target_ref, colour_ref, out_ref,
+    table, onehot, coef, power_w, diff_w, alpha, weight, weight_h, weight_l, pull,
+    dp_h, dp_m, dp_l, spread, total, mono,
+):
+    groups, _, rows = slots_ref.shape
+    slots = rows // 8
+    for feat in range(9):
+        block = jnp.concatenate(
+            [recv_ref[16 * j : 16 * j + 16, 64 * feat : 64 * feat + 64] for j in range(4)], axis=1
+        )
+        for part, piece in enumerate(split3(block)):
+            table[pl.ds((part * 9 + feat) * 16, 16), :] = piece
+    total[...] = jnp.zeros_like(total)
+    coef[...] = jnp.zeros_like(coef)
+    diff_w[...] = jnp.zeros_like(diff_w)
+    pixel = iota((16, 256), 1)
+    off_u = (pixel & 15).astype(F32) - 7.5
+    off_v = (pixel >> 4).astype(F32) - 7.5
+    which = iota((16, 256), 0)
+    def pick(kind, u, v):
+        out = jnp.where(kind == 0, 1.0, 0.0)
+        out = jnp.where(kind == 1, u, out)
+        out = jnp.where(kind == 2, v, out)
+        out = jnp.where(kind == 3, u * u, out)
+        out = jnp.where(kind == 4, u * v, out)
+        return jnp.where(kind == 5, v * v, out)
+    mono[...] = pick(which, off_u, off_v).astype(BF16)
+    row = iota((128, 256), 0)
+    pix = iota((128, 256), 1)
+    kind = jnp.where(row >= 12, row - 12, jnp.where(row >= 6, row - 6, row))
+    power_w[...] = jnp.where(
+        row < 18,
+        pick(kind, (pix & 15).astype(F32) - 7.5, (pix >> 4).astype(F32) - 7.5),
         0.0,
-    ).astype(jnp.float32)
-    passed = jnp.exp(jnp.einsum("bps,sk->bpk", log_keep, earlier, precision=lax.Precision.HIGHEST))
-    weight = passed * alpha
-    return jnp.einsum("bps,cbs->bcp", weight, features[6:9], precision=lax.Precision.HIGHEST)
-
-
-def render_tiles(features, slot_rows, tile_ids, target):
+    ).astype(BF16)
+
+    lane_tile = iota((1, rows), 1) & 7
+    own = iota((8, rows), 0) == lane_tile
+    hi_row = iota((16, rows), 0)
+
+    def group(step, carry):
+        index = slots_ref[step]
+        live = index >= 0
+        low = ((index >> 10) << 6) | (index & 63)
+        high = jnp.where(live, (index >> 6) & 15, -1)
+        onehot[...] = jnp.where(iota((256, rows), 0) == low, 1.0, 0.0).astype(BF16)
+        mask = hi_row == high
+        raw = dot(table[...], onehot[...])
+        feats = []
+        for feat in range(9):
+            part = (
+                raw[288 + 16 * feat : 304 + 16 * feat] + raw[144 + 16 * feat : 160 + 16 * feat]
+            ) + raw[16 * feat : 16 * feat + 16]
+            feats.append(jnp.sum(jnp.where(mask, part, 0.0), axis=0, keepdims=True))
+        mean_x, mean_y, con_a, con_b, con_c, log_op = feats[:6]
+        centre_x = jnp.zeros((1, rows), F32)
+        centre_y = jnp.zeros((1, rows), F32)
+        for t in range(8):
+            tid = tid_ref[0, step * 8 + t]
+            centre_x = jnp.where(lane_tile == t, ((tid & 15) * 16 + 8).astype(F32), centre_x)
+            centre_y = jnp.where(lane_tile == t, ((tid >> 4) * 16 + 8).astype(F32), centre_y)
+        far_x = centre_x - mean_x
+        far_y = centre_y - mean_y
+        ax = con_a * far_x
+        bx = con_b * far_x
+        by = con_b * far_y
+        cy = con_c * far_y
+        constant = far_x * (ax + by) + far_y * cy + log_op
+        constant = jnp.where(live, constant, -1e30)
+        for m, value in enumerate(
+            (constant, 2.0 * ax + by, bx + 2.0 * cy, con_a, con_b, con_c)
+        ):
+            for part, piece in enumerate(split3(value)):
+                coef[pl.ds(part * 6 + m, 1), :] = piece.astype(F32)
+        for ch in range(3):
+            c_high, c_mid = split2(feats[6 + ch])
+            c_high = jnp.where(own, c_high.astype(F32), 0.0)
+            coef[24 + 8 * ch : 32 + 8 * ch, :] = c_high
+            coef[48 + 8 * ch : 56 + 8 * ch, :] = jnp.where(own, c_mid.astype(F32), 0.0)
+            coef[72 + 8 * ch : 80 + 8 * ch, :] = c_high
+        turned = jnp.transpose(coef[...]).astype(BF16)
+        alpha[...] = dot(turned, power_w[...])
+
+        def forward(chunk, passed):
+            base = pl.multiple_of(chunk * 128, 128)
+            powers = alpha[pl.ds(base, 128), :]
+            alphas = jnp.exp2(powers)
+            alpha[pl.ds(base, 128), :] = alphas
+            out = []
+            for k in range(16):
+                w = passed * alphas[8 * k : 8 * k + 8]
+                passed = passed - w
+                out.append(w)
+            out = jnp.concatenate(out, axis=0)
+            weight[pl.ds(base, 128), :] = out
+            w_h, w_l = split2(out)
+            weight_h[pl.ds(base, 128), :] = w_h
+            weight_l[pl.ds(base, 128), :] = w_l
+            return passed
+
+        lax.fori_loop(0, slots // 16, forward, jnp.ones((8, 256), F32))
+        tinted = coef[24:72, :].astype(BF16)
+        first = dot(tinted, weight_h[...])
+        second = dot(tinted, weight_l[...])
+        shown = first[:24] + (first[24:48] + second[:24])
+        diffs_h, diffs_m = [], []
+        for ch in range(3):
+            colour = shown[8 * ch : 8 * ch + 8]
+            where = pl.ds(pl.multiple_of(step * 8, 8), 8)
+            colour_ref[ch, where, :] = colour
+            d_high, d_mid = split2(colour - target_ref[ch, where, :])
+            d_high = d_high.astype(F32)
+            diffs_h.append(d_high)
+            diffs_m.append(d_mid.astype(F32))
+            diff_w[24 + 8 * ch : 32 + 8 * ch, :] = d_high
+            diff_w[48 + 8 * ch : 56 + 8 * ch, :] = d_high
+            diff_w[72 + 8 * ch : 80 + 8 * ch, :] = d_mid.astype(F32)
+        pull[...] = dot(turned, diff_w[...].astype(BF16))
+
+        def backward(chunk, behind):
+            base = pl.multiple_of((slots // 16 - 1 - chunk) * 128, 128)
+            alphas = alpha[pl.ds(base, 128), :]
+            weights = weight[pl.ds(base, 128), :]
+            pulls = pull[pl.ds(base, 128), :]
+            out = [None] * 16
+            for k in range(15, -1, -1):
+                gap = pulls[8 * k : 8 * k + 8] - behind
+                out[k] = weights[8 * k : 8 * k + 8] * gap
+                behind = behind + alphas[8 * k : 8 * k + 8] * gap
+            out = jnp.concatenate(out, axis=0)
+            d_h, d_m, d_l = split3(out)
+            dp_h[pl.ds(base, 128), :] = d_h
+            dp_m[pl.ds(base, 128), :] = d_m
+            dp_l[pl.ds(base, 128), :] = d_l
+            return behind
+
+        lax.fori_loop(0, slots // 16, backward, jnp.zeros((8, 256), F32))
+        diff48 = diff_w[48:96, :].astype(BF16)
+        tint_h = dot(diff48, weight_h[...], NT)
+        tint_l = dot(diff48, weight_l[...], NT)
+        tint = tint_h[:24] + (tint_h[24:48] + tint_l[:24])
+        moments = (
+            dot(mono[...], dp_l[...], NT) + dot(mono[...], dp_m[...], NT)
+        ) + dot(mono[...], dp_h[...], NT)
+        s_0, s_u, s_v, s_uu, s_uv, s_vv = [LN2 * moments[m : m + 1] for m in range(6)]
+        sum_x = far_x * s_0 + s_u
+        sum_y = far_y * s_0 + s_v
+        grads = [
+            -(2.0 * con_a * sum_x + con_b * sum_y),
+            -(con_b * sum_x + 2.0 * con_c * sum_y),
+            far_x * (sum_x + s_u) + s_uu,
+            far_x * sum_y + far_y * s_u + s_uv,
+            far_y * (sum_y + s_v) + s_vv,
+            s_0,
+        ] + [
+            jnp.sum(jnp.where(own, tint[8 * ch : 8 * ch + 8], 0.0), axis=0, keepdims=True)
+            for ch in range(3)
+        ]
+        for feat in range(9):
+            for part, piece in enumerate(split3(grads[feat])):
+                spread[pl.ds((part * 9 + feat) * 16, 16), :] = jnp.where(
+                    mask, piece.astype(F32), 0.0
+                ).astype(BF16)
+        total[...] += dot(spread[...], onehot[...], NT)
+        return carry
+
+    lax.fori_loop(0, groups, group, 0)
+    for feat in range(9):
+        grid = (
+            total[16 * feat + 288 : 16 * feat + 304] + total[16 * feat + 144 : 16 * feat + 160]
+        ) + total[16 * feat : 16 * feat + 16]
+        for j in range(4):
+            out_ref[16 * j : 16 * j + 16, 64 * feat : 64 * feat + 64] = grid[
+                :, 64 * j : 64 * j + 64
+            ]
+    out_ref[:, 576:640] = jnp.zeros((64, 64), F32)
+
+
+def render(recv, slot_rows, tile_ids, target):
     tiles, slots = slot_rows.shape
-    width = features.shape[0]
-    live = slot_rows >= 0
-    safe = jnp.where(live, slot_rows, 0)
-    live_float = jnp.where(live, 1.0, 0.0).astype(jnp.float32)
-    gathered = jnp.take(features, safe.reshape(-1), axis=1).reshape(width, tiles, slots)
-    lane = lax.iota(jnp.int32, TILE * TILE)
-    pix_x = (tile_ids[:, None] % IMG_TILES * TILE + lane[None, :] % TILE).astype(jnp.float32) + 0.5
-    pix_y = (tile_ids[:, None] // IMG_TILES * TILE + lane[None, :] // TILE).astype(
-        jnp.float32
-    ) + 0.5
-    groups = tiles // 4
-    stacked = (
-        gathered.reshape(width, groups, 4, slots).transpose(1, 0, 2, 3),
-        live_float.reshape(groups, 4, slots),
-        pix_x.reshape(groups, 4, -1),
-        pix_y.reshape(groups, 4, -1),
-        target.reshape(groups, 4, 3, -1),
-    )
-
-    def shade(block):
-        feats_block, live_block, across, down, wanted = block
-        colour, pull = jax.vjp(
-            lambda part_feats: blend(part_feats, live_block, across, down), feats_block
-        )
-        (slot_grad,) = pull(colour - wanted)
-        return (colour, slot_grad)
-
-    colours, grads = lax.map(shade, stacked)
-    slot_grads = grads.transpose(1, 0, 2, 3).reshape(width, tiles * slots)
-    row_grads = jax.ops.segment_sum(
-        slot_grads.T, safe.reshape(-1), num_segments=features.shape[1]
-    ).T
-    return (colours.reshape(tiles, 3, -1), row_grads)
+    groups = tiles // 8
+    rows = slots * 8
+    ordered = slot_rows.reshape(groups, 8, slots).transpose(0, 2, 1).reshape(groups, 1, rows)
+    vm = lambda *shape_type: pltpu.VMEM(*shape_type)
+    return pl.pallas_call(
+        render_kernel,
+        out_shape=(
+            jax.ShapeDtypeStruct((3, tiles, 256), F32),
+            jax.ShapeDtypeStruct((64, 640), F32),
+        ),
+        in_specs=[
+            pl.BlockSpec(memory_space=pltpu.SMEM),
+            pl.BlockSpec(memory_space=pltpu.VMEM),
+            pl.BlockSpec(memory_space=pltpu.VMEM),
+            pl.BlockSpec(memory_space=pltpu.VMEM),
+        ],
+        out_specs=(
+            pl.BlockSpec(memory_space=pltpu.VMEM),
+            pl.BlockSpec(memory_space=pltpu.VMEM),
+        ),
+        scratch_shapes=[
+            vm((432, 256), BF16),
+            vm((256, rows), BF16),
+            vm((128, rows), F32),
+            vm((128, 256), BF16),
+            vm((128, 256), F32),
+            vm((rows, 256), F32),
+            vm((rows, 256), F32),
+            vm((rows, 256), BF16),
+            vm((rows, 256), BF16),
+            vm((rows, 256), F32),
+            vm((rows, 256), BF16),
+            vm((rows, 256), BF16),
+            vm((rows, 256), BF16),
+            vm((432, rows), BF16),
+            vm((432, 256), F32),
+            vm((16, 256), BF16),
+        ],
+        compiler_params=pltpu.CompilerParams(vmem_limit_bytes=56 * 1024 * 1024),
+        name="render",
+    )(tile_ids, recv, ordered, target)
 
 
 def adam_update(params, adam_m, adam_v, gradient):
@@ -214,29 +407,48 @@
     return (new_params, new_m, new_v)
 
 
+def sent_features(raw, camera):
+    feats = project(raw, camera)
+    log2_e = 1.0 / LN2
+    return jnp.stack(
+        [
+            feats[0],
+            feats[1],
+            (-0.5 * log2_e) * feats[2],
+            -log2_e * feats[3],
+            (-0.5 * log2_e) * feats[4],
+            jnp.log(feats[5]) * log2_e,
+            feats[6],
+            feats[7],
+            feats[8],
+        ]
+    )
+
+
 def on_device(
     params, adam_m, adam_v, cameras, device_camera, send_index, slot_rows, tile_ids, target
 ):
-    n_gs = lax.axis_size("gs")
-    capacity = send_index.shape[-1]
-    width = params.shape[0]
     local = send_index[0, 0].reshape(-1)
-    outgoing = jnp.take(params, local, axis=1)
+    raw = jnp.take(params, local, axis=1).reshape(-1, 32, 128)
     dest_cameras = jnp.take(cameras, device_camera[0], axis=1)
-    own_camera = jnp.take(dest_cameras, lax.axis_index("gs")[None], axis=1)
-    incoming = lax.all_to_all(
-        outgoing.reshape(width, n_gs, capacity), "gs", split_axis=1, concat_axis=1, tiled=True
-    ).reshape(width, -1)
-    features, pull = jax.vjp(lambda raw: project(raw, own_camera), incoming)
-    colours, row_grads = render_tiles(features, slot_rows[0, 0], tile_ids[0, 0], target[0, 0])
-    (raw_grads,) = pull(row_grads)
-    sent_grads = lax.all_to_all(
-        raw_grads.reshape(width, n_gs, capacity), "gs", split_axis=1, concat_axis=1, tiled=True
-    ).reshape(width, -1)
-    gradient = jax.ops.segment_sum(sent_grads.T, local, num_segments=params.shape[1]).T
+    camera = jnp.repeat(dest_cameras, 64, axis=1).reshape(16, 32, 128)
+    features, pull = jax.vjp(lambda rows: sent_features(rows, camera), raw)
+    outgoing = features.reshape(9, 64, 64).transpose(1, 0, 2).reshape(64, 576)
+    incoming = lax.all_to_all(outgoing, "gs", 0, 0, tiled=True)
+    colours, back = render(
+        jnp.pad(incoming, ((0, 0), (0, 64))),
+        slot_rows[0, 0],
+        tile_ids[0],
+        target[0, 0].transpose(1, 0, 2),
+    )
+    returned = lax.all_to_all(back[:, :576], "gs", 0, 0, tiled=True)
+    (raw_grads,) = pull(returned.reshape(64, 9, 64).transpose(1, 0, 2).reshape(9, 32, 128))
+    gradient = jax.ops.segment_sum(
+        raw_grads.reshape(59, -1).T, local, num_segments=params.shape[1]
+    ).T
     total = lax.psum(gradient, "img")
     new_params, new_m, new_v = adam_update(params, adam_m, adam_v, total)
-    return (new_params, new_m, new_v, colours[None, None])
+    return (new_params, new_m, new_v, colours.transpose(1, 0, 2)[None, None])
 
 
 def solution(mesh):

time: 485 us -> 200 us (0.41); the launches traced: 478 us -> 200 us
  other arithmetic: 146 us -> 35.3 us
  matrix products: 93 us -> 0 us
  local copies, waits for them, and re-layouts: 110 us -> 40.2 us
  Pallas kernels: 0 us -> 29.9 us
  waiting for transfers between devices: 88.1 us -> 60.6 us
  between operations: 20.1 us -> 15 us
    dot_general x40 -> x0, matrix products: 93 us -> none  [the longest x16 47.2 us: blend(): jnp.einsum('bps,sk->bpk', log_keep, earlier, precision=lax.Precision.HIGH...]
    scatter-add x2 -> x1, other arithmetic: 78.4 us -> 23.2 us  [on_device(): jax.ops.segment_sum(raw_grads.reshape(59, -1).T, local, num_segments=para...]
    gather x4 -> x2, local copies, waits for them, and re-layouts: 49.5 us -> 16.3 us  [on_device(): raw = jnp.take(params, local, axis=1).reshape(-1, 32, 128)]
    pallas_call x0 -> x1, Pallas kernels: none -> 29.9 us  [render(): pl.pallas_call(render_kernel, out_shape=(jax.ShapeDtypeStruct((3, tiles,...]
    all_to_all x2, waiting for transfers between devices: 39.5 us -> 12.6 us  [the longest x1 8.19 us: on_device(): incoming = lax.all_to_all(outgoing, 'gs', 0, 0, tiled=True)]
    squeeze x45, local copies, waits for them, and re-layouts: 15.2 us -> 3.2 us  [project(): raw[11 + 3 * term + channel]]
    mul x12 -> x3, other arithmetic: 10.8 us -> 0.01 us  [project(): jacobian[first][inner] * turn[inner][second]]
    unnamed x154 -> x54, local copies, waits for them, and re-layouts: 11 us -> 2.06 us
  transfers between devices with their start and end apart: 3 -> 3, of which waited for: 3 -> 3; matrix products, arithmetic and copies ran while one was open for 2% -> 3% of each run, Pallas kernels for 0% -> 0%
where the time goes in v1:
time: 200 us
  waiting for transfers between devices  60.6 us (30%)
  local copies, waits for them, and re-layouts  40.2 us (20%)
  other arithmetic  35.3 us (18%)
  Pallas kernels  29.9 us (15%)
  starting transfers between devices  18.6 us (9%)
  between operations  15 us (8%)
    psum x1, waiting for transfers between devices, on_device(): total = lax.psum(gradient, 'img')  48 us
    pallas_call x1, Pallas kernels, render(): pl.pallas_call(render_kernel, out_shape=(jax.ShapeDtypeStruct((3, tiles,...  29.9 us
    scatter-add x1, other arithmetic, on_device(): jax.ops.segment_sum(raw_grads.reshape(59, -1).T, local, num_segments=para...  23.2 us
    gather x2, local copies, waits for them, and re-layouts, on_device(): raw = jnp.take(params, local, axis=1).reshape(-1, 32, 128)  16.3 us
    all_to_all x1, starting transfers between devices, on_device(): incoming = lax.all_to_all(outgoing, 'gs', 0, 0, tiled=True)  12.1 us
    all_to_all x1, waiting for transfers between devices, on_device(): incoming = lax.all_to_all(outgoing, 'gs', 0, 0, tiled=True)  8.19 us
    all_to_all x1, starting transfers between devices, on_device(): returned = lax.all_to_all(back[:, :576], 'gs', 0, 0, tiled=True)  6.2 us
    broadcast_in_dim x48, local copies, waits for them, and re-layouts, on_device(): camera = jnp.repeat(dest_cameras, 64, axis=1).reshape(16, 32, 128)  4.41 us
  transfers between devices with their start and end apart: 3, of which 3 were waited for; matrix products, arithmetic and copies ran while one was open for 3% of the time, Pallas kernels for 0%

profile of v1, /device:TPU:8, one launch (start us, length us, event | category | flops | bytes accessed | tf_op | source)
XLA Modules:
  0.0 199.6 jit_solution(14048288139829004044)
XLA Ops:
  7.2 0.7 fusion.58
  7.8 0.7 compare_and_fusion.1
  8.5 0.8 reshape.16625
  9.3 0.8 broadcast_in_dim_reshape_squeeze.3
  10.2 1.9 copy.138
  12.1 14.1 %gather_fusion.1 = f32[4096,59]{1,0:T(8,128)} fusion(f32[59,4096]{0,1:T(8,128)S(1)} %copy.138, s32[4096]{0:T(1024)S(1)} %broadcast_clamp_fusion), kind=kCustom, calls=%fused_computation.1 | custom fusion | bytes 1949696 | tf_op jit(solution)/shard_map/jit(_take)/gather | solution.py:432
  26.2 2.2 %copy.139 = f32[4096,59]{0,1:T(8,128)S(1)} copy(f32[4096,59]{1,0:T(8,128)} %gather_fusion.1) | data formatting | bytes 1933312 | tf_op jit(solution)/shard_map/jit(_take)/gather | solution.py:432
  28.5 0.8 slice_reduce_fusion.30
  29.3 0.2 fusion.109
  29.5 0.8 slice_reduce_fusion.29
  30.2 0.8 slice_reduce_fusion.28
  31.0 0.4 slice_reduce_fusion.19
  31.5 0.6 gather_fusion
  32.2 1.1 slice_reduce_fusion.2
  34.0 0.2 multiply_add_fusion.4
  34.2 0.2 multiply_add_fusion.3
  34.4 0.2 multiply_add_fusion.10
  34.6 0.2 multiply_add_fusion.9
  34.8 0.2 multiply_dynamic-update-slice_fusion.2
  38.6 0.9 maximum_dynamic-update-slice_fusion.2
  39.5 0.1 maximum_dynamic-update-slice_fusion.1
  39.6 0.1 maximum_dynamic-update-slice_fusion
  39.7 0.1 copy.140
  39.8 0.8 copy.141
  40.6 12.1 %all-to-all-start = ((f32[64,1,576]{2,1,0:T(1,128)}), f32[64,1,576]{2,1,0:T(1,128)S(1)}, u32[]{:S(2)}, u32[]{:S(2)}) async-start(f32[64,1,576]{2,1,0:T(1,128)} %copy.141), calls=%async_computation | async-start | bytes 327680 | tf_op jit(solution)/shard_map/all_to_all | solution.py:437
  52.8 0.3 fusion.107
  53.2 0.2 copy.142
  53.4 0.9 reshape.16632.slots_ref
  54.3 8.2 %all-to-all-done = f32[64,1,576]{2,1,0:T(1,128)S(1)} async-done(((f32[64,1,576]{2,1,0:T(1,128)}), f32[64,1,576]{2,1,0:T(1,128)S(1)}, u32[]{:S(2)}, u32[]{:S(2)}) %all-to-all-start) | async-done | bytes 147488 | tf_op jit(solution)/shard_map/all_to_all | solution.py:437
  62.5 0.7 pad.224.recv_ref
  63.2 29.9 %render.1 = (f32[3,32,256]{2,1,0:T(8,128)}, f32[64,640]{1,0:T(8,128)}) custom-call(s32[1,32]{1,0:T(1,128)} %bitcast.317, f32[64,640]{1,0:T(8,128)} %pad.224.recv_ref, s32[4,1,2048]{2,1,0:T(1,128)} %reshape.16632.slots_ref, f32[3,32,256]{2,1,0:T(8,128)} %bitcast.311), custom_call_target="tpu_custom_call" | custom-call | tf_op jit(solution)/shard_map/render/pallas_call | solution.py:363
  93.1 0.9 slice_bitcast_fusion
  94.0 0.8 copy.144
  94.9 6.2 %all-to-all-start.1 = ((f32[64,1,576]{2,1,0:T(1,128)}), f32[64,1,576]{2,1,0:T(1,128)S(1)}, u32[]{:S(2)}, u32[]{:S(2)}) async-start(f32[64,1,576]{2,1,0:T(1,128)} %copy.144), calls=%async_computation.1 | async-start | bytes 327680 | tf_op jit(solution)/shard_map/all_to_all | solution.py:444
  101.1 0.3 all-reduce.75.cloned.1.call-start
  101.3 0.3 fusion.108
  101.6 0.1 broadcast_in_dim.251
  101.8 0.1 broadcast_in_dim.254
  101.9 0.1 broadcast_in_dim.257
  102.0 0.1 broadcast_in_dim.260
  102.1 0.1 broadcast_in_dim.263
  102.2 0.1 broadcast_in_dim.266
  102.3 0.1 broadcast_in_dim.275
  102.4 0.1 broadcast_in_dim.281
  102.5 0.1 broadcast_in_dim.284
  102.6 0.1 broadcast_in_dim.278
  102.7 0.1 broadcast_in_dim.290
  102.9 0.1 broadcast_in_dim.293
  103.0 0.1 broadcast_in_dim.272
  106.4 4.4 %all-to-all-done.1 = f32[64,1,576]{2,1,0:T(1,128)S(1)} async-done(((f32[64,1,576]{2,1,0:T(1,128)}), f32[64,1,576]{2,1,0:T(1,128)S(1)}, u32[]{:S(2)}, u32[]{:S(2)}) %all-to-all-start.1) | async-done | bytes 147488 | tf_op jit(solution)/shard_map/all_to_all | solution.py:444
  110.8 0.2 copy.145
  111.0 0.1 copy.146
  112.1 0.1 fusion.43
  112.2 0.2 multiply_add_fusion.59
  112.4 0.1 rsqrt_multiply_fusion.9
  112.5 0.3 fusion.23
  112.8 0.2 fusion.26
  113.0 0.2 fusion.29
  113.4 0.5 fusion.8
  113.9 2.1 %copy.149 = f32[59,32,128]{0,2,1:T(8,128)} copy(f32[59,32,128]{2,1,0:T(8,128)S(1)} %fusion.8) | data formatting | bytes 1933312 | tf_op jit(solution)/shard_map/reshape | solution.py:447
  116.0 23.2 %scatter_custom_fusion = f32[4096,59]{1,0:T(8,128)S(1)} fusion(s32[4096]{0:T(1024)S(1)} %reshape.16625, f32[4096,59]{1,0:T(8,128)} %bitcast.97, f32[]{:T(128)} %constant.42.clone.1), kind=kCustom, calls=%fused_computation.12 | custom fusion | flops 241664 | bytes 967168 | tf_op jit(solution)/shard_map/scatter-add | solution.py:446
  139.2 1.6 copy.148
  140.8 48.0 %all-reduce.75.cloned.1.call-done = f32[59,4096]{1,0:T(8,128)} async-done(((f32[59,4096]{1,0:T(8,128)}), f32[59,4096]{1,0:T(8,128)}) %all-reduce.75.cloned.1.call-update) | async-done | bytes 966672 | tf_op jit(solution)/shard_map/psum | solution.py:449
  188.8 3.9 %divide_subtract_fusion = (f32[59,4096]{1,0:T(8,128)}, f32[59,4096]{1,0:T(8,128)}, f32[59,4096]{1,0:T(8,128)}) fusion(f32[59,4096]{1,0:T(8,128)S(1)} %copy-done, f32[59]{0:T(128)S(1)} %copy-done.24, f32[59,4096]{1,0:T(8,128)} %all-reduce.75.cloned.1.call-done, f32[59,4096]{1,0:T(8,128)} %param.11, f32[59,4096]{1,0:T(8,128)} %param.12), kind=kLoop, calls=%fused_computation.10 | loop fusion | flops 2899968 | bytes 6766828 | tf_op jit(solution)/shard_map/sub | solution.py:406
  (181 shorter events, 9.0 us)
Async XLA Ops:
  28.4 3.0 %copy-start.14 = (f32[16,16]{1,0:T(8,128)S(1)}, f32[16,16]{1,0:T(8,128)}, u32[]{:S(2)}) copy-start(f32[16,16]{1,0:T(8,128)} %param.13) | copy-start | bytes 3076
  33.2 1.0 copy-start.15
  33.2 1.0 copy-start.19
  33.2 3.3 %copy-start.2 = (f32[64]{0:T(128)}, f32[64]{0:T(128)S(1)}, u32[]{:S(2)}) copy-start(f32[64]{0:T(128)S(1)} %get-tuple-element.83) | copy-start | bytes 772
  33.2 3.3 %copy-start.4 = (f32[64]{0:T(128)}, f32[64]{0:T(128)S(1)}, u32[]{:S(2)}) copy-start(f32[64]{0:T(128)S(1)} %get-tuple-element.84) | copy-start | bytes 772
  33.2 3.3 %copy-start.6 = (f32[64]{0:T(128)}, f32[64]{0:T(128)S(1)}, u32[]{:S(2)}) copy-start(f32[64]{0:T(128)S(1)} %get-tuple-element.85) | copy-start | bytes 772
  33.2 3.3 %copy-start.8 = (f32[64]{0:T(128)}, f32[64]{0:T(128)S(1)}, u32[]{:S(2)}) copy-start(f32[64]{0:T(128)S(1)} %get-tuple-element.91) | copy-start | bytes 772
  33.2 3.3 %copy-start.10 = (f32[64]{0:T(128)}, f32[64]{0:T(128)S(1)}, u32[]{:S(2)}) copy-start(f32[64]{0:T(128)S(1)} %get-tuple-element.92) | copy-start | bytes 772
  33.3 3.3 %copy-start.12 = (f32[64]{0:T(128)}, f32[64]{0:T(128)S(1)}, u32[]{:S(2)}) copy-start(f32[64]{0:T(128)S(1)} %get-tuple-element.93) | copy-start | bytes 772
  33.3 3.3 %copy-start.17 = (f32[64]{0:T(128)}, f32[64]{0:T(128)S(1)}, u32[]{:S(2)}) copy-start(f32[64]{0:T(128)S(1)} %get-tuple-element.82) | copy-start | bytes 772
  38.5 14.7 %copy-start.1 = (s32[1,1,32,256]{3,2,1,0:T(8,128)S(1)}, s32[1,1,32,256]{3,2,1,0:T(8,128)}, u32[]{:S(2)}) copy-start(s32[1,1,32,256]{3,2,1,0:T(8,128)} %param.16) | copy-start | bytes 98308
  40.6 21.9 %all-to-all-start = ((f32[64,1,576]{2,1,0:T(1,128)}), f32[64,1,576]{2,1,0:T(1,128)S(1)}, u32[]{:S(2)}, u32[]{:S(2)}) async-start(f32[64,1,576]{2,1,0:T(1,128)} %copy.141), calls=%async_computation | async-start | bytes 327680 | tf_op jit(solution)/shard_map/all_to_all | solution.py:437
  52.8 48.9 %copy-start.23 = (f32[64]{0:T(128)S(1)}, f32[64]{0:T(128)}, u32[]{:S(2)}) copy-start(f32[64]{0:T(128)} %get-tuple-element.81) | copy-start | bytes 772
  52.8 49.0 %copy-start.22 = (f32[64]{0:T(128)S(1)}, f32[64]{0:T(128)}, u32[]{:S(2)}) copy-start(f32[64]{0:T(128)} %get-tuple-element.78) | copy-start | bytes 772
  52.8 49.1 %copy-start.21 = (f32[64]{0:T(128)S(1)}, f32[64]{0:T(128)}, u32[]{:S(2)}) copy-start(f32[64]{0:T(128)} %get-tuple-element.80) | copy-start | bytes 772
  52.8 49.6 %copy-start.7 = (f32[64]{0:T(128)S(1)}, f32[64]{0:T(128)}, u32[]{:S(2)}) copy-start(f32[64]{0:T(128)} %copy-done.6) | copy-start | bytes 772
  52.8 49.7 %copy-start.5 = (f32[64]{0:T(128)S(1)}, f32[64]{0:T(128)}, u32[]{:S(2)}) copy-start(f32[64]{0:T(128)} %copy-done.4) | copy-start | bytes 772
  52.8 49.8 %copy-start.3 = (f32[64]{0:T(128)S(1)}, f32[64]{0:T(128)}, u32[]{:S(2)}) copy-start(f32[64]{0:T(128)} %copy-done.2) | copy-start | bytes 772
  52.8 49.9 %copy-start.13 = (f32[64]{0:T(128)S(1)}, f32[64]{0:T(128)}, u32[]{:S(2)}) copy-start(f32[64]{0:T(128)} %copy-done.12) | copy-start | bytes 772
  52.8 50.0 %copy-start.11 = (f32[64]{0:T(128)S(1)}, f32[64]{0:T(128)}, u32[]{:S(2)}) copy-start(f32[64]{0:T(128)} %copy-done.10) | copy-start | bytes 772
  53.1 49.8 %copy-start.9 = (f32[64]{0:T(128)S(1)}, f32[64]{0:T(128)}, u32[]{:S(2)}) copy-start(f32[64]{0:T(128)} %copy-done.8) | copy-start | bytes 772
  53.1 49.9 %copy-start.20 = (f32[64]{0:T(128)S(1)}, f32[64]{0:T(128)}, u32[]{:S(2)}) copy-start(f32[64]{0:T(128)} %copy-done.19) | copy-start | bytes 772
  53.2 50.0 %copy-start.18 = (f32[64]{0:T(128)S(1)}, f32[64]{0:T(128)}, u32[]{:S(2)}) copy-start(f32[64]{0:T(128)} %copy-done.17) | copy-start | bytes 772
  53.2 50.1 %copy-start.16 = (f32[64]{0:T(128)S(1)}, f32[64]{0:T(128)}, u32[]{:S(2)}) copy-start(f32[64]{0:T(128)} %copy-done.15) | copy-start | bytes 772
  94.9 15.9 %all-to-all-start.1 = ((f32[64,1,576]{2,1,0:T(1,128)}), f32[64,1,576]{2,1,0:T(1,128)S(1)}, u32[]{:S(2)}, u32[]{:S(2)}) async-start(f32[64,1,576]{2,1,0:T(1,128)} %copy.144), calls=%async_computation.1 | async-start | bytes 327680 | tf_op jit(solution)/shard_map/all_to_all | solution.py:444
  101.1 87.7 %all-reduce.75.cloned.1.call-start = ((), (), s32[]{:S(2)}) async-start(), calls=%async_computation.2 | async-start | bytes 2097152 | tf_op jit(solution)/shard_map/psum | solution.py:449
  139.2 49.6 %copy-start = (f32[59,4096]{1,0:T(8,128)S(1)}, f32[59,4096]{1,0:T(8,128)}, u32[]{:S(2)}) copy-start(f32[59,4096]{1,0:T(8,128)} %param.10) | copy-start | bytes 2899972
  139.2 49.6 %copy-start.24 = (f32[59]{0:T(128)S(1)}, f32[59]{0:T(128)}, u32[]{:S(2)}) copy-start(f32[59]{0:T(128)} %constant.258) | copy-start | bytes 712
Sparse Core Ops, SparseCore 0:
  140.9 47.8 all-reduce.74

commit v2 on v1

--- a/solution.py
+++ b/solution.py
@@ -31,6 +31,9 @@
 learn_rates = np.array(
     [0.00016] * 3 + [0.005] * 3 + [0.001] * 4 + [0.05] + [0.0025] * 3 + [0.000125] * 45
 )
+LN2 = float(np.log(2.0))
+LOG2_E = 1.0 / LN2
+LOG_TOP = float(np.log2(0.99))
 bias_first = 1.0 - 0.9**10
 bias_second = 1.0 - 0.999**10
 
@@ -59,7 +62,7 @@
     ]
 
 
-def project(raw, camera):
+def sent_features(raw, camera):
     world = [raw[0], raw[1], raw[2]]
     scales = [jnp.exp(raw[3]), jnp.exp(raw[4]), jnp.exp(raw[5])]
     quat_sq = jnp.maximum(
@@ -134,25 +137,24 @@
         )
         for channel in range(3)
     ]
-    return jnp.stack(
-        [
-            focal * viewed[0] * inv_depth + half_width,
-            focal * viewed[1] * inv_depth + half_width,
-            cov_yy / determinant,
-            -cov_xy / determinant,
-            cov_xx / determinant,
-            0.99 * jax.nn.sigmoid(raw[10]),
-            colours[0],
-            colours[1],
-            colours[2],
-        ]
-    )
+    inverse_det = 1.0 / determinant
+    log_opacity = LOG_TOP - jnp.log(1.0 + jnp.exp(-raw[10])) * LOG2_E
+    return [
+        focal * viewed[0] * inv_depth + half_width,
+        focal * viewed[1] * inv_depth + half_width,
+        (-0.5 * LOG2_E) * cov_yy * inverse_det,
+        LOG2_E * cov_xy * inverse_det,
+        (-0.5 * LOG2_E) * cov_xx * inverse_det,
+        log_opacity,
+        colours[0],
+        colours[1],
+        colours[2],
+    ]
 
 
 F32, BF16, I32 = jnp.float32, jnp.bfloat16, jnp.int32
 NN = (((1,), (0,)), ((), ()))
 NT = (((1,), (1,)), ((), ()))
-LN2 = float(np.log(2.0))
 
 
 def dot(left, right, dims=NN):
@@ -183,8 +185,10 @@
     groups, _, rows = slots_ref.shape
     slots = rows // 8
     for feat in range(9):
+        side = slice(64 * (feat % 2), 64 * (feat % 2) + 64)
         block = jnp.concatenate(
-            [recv_ref[16 * j : 16 * j + 16, 64 * feat : 64 * feat + 64] for j in range(4)], axis=1
+            [recv_ref[pl.ds(80 * j + feat // 2, 16, stride=5), :][:, side] for j in range(4)],
+            axis=1,
         )
         for part, piece in enumerate(split3(block)):
             table[pl.ds((part * 9 + feat) * 16, 16), :] = piece
@@ -343,15 +347,19 @@
         return carry
 
     lax.fori_loop(0, groups, group, 0)
+    grids = []
     for feat in range(9):
-        grid = (
-            total[16 * feat + 288 : 16 * feat + 304] + total[16 * feat + 144 : 16 * feat + 160]
-        ) + total[16 * feat : 16 * feat + 16]
+        grids.append(
+            (total[16 * feat + 288 : 16 * feat + 304] + total[16 * feat + 144 : 16 * feat + 160])
+            + total[16 * feat : 16 * feat + 16]
+        )
+    grids.append(jnp.zeros((16, 256), F32))
+    for pair in range(5):
         for j in range(4):
-            out_ref[16 * j : 16 * j + 16, 64 * feat : 64 * feat + 64] = grid[
-                :, 64 * j : 64 * j + 64
-            ]
-    out_ref[:, 576:640] = jnp.zeros((64, 64), F32)
+            lanes = slice(64 * j, 64 * j + 64)
+            out_ref[pl.ds(80 * j + pair, 16, stride=5), :] = jnp.concatenate(
+                [grids[2 * pair][:, lanes], grids[2 * pair + 1][:, lanes]], axis=1
+            )
 
 
 def render(recv, slot_rows, tile_ids, target):
@@ -364,7 +372,7 @@
         render_kernel,
         out_shape=(
             jax.ShapeDtypeStruct((3, tiles, 256), F32),
-            jax.ShapeDtypeStruct((64, 640), F32),
+            jax.ShapeDtypeStruct((320, 128), F32),
         ),
         in_specs=[
             pl.BlockSpec(memory_space=pltpu.SMEM),
@@ -399,6 +407,174 @@
     )(tile_ids, recv, ordered, target)
 
 
+def camera_block(camera_ref, chosen_ref, block):
+    lane = iota((8, 128), 1)
+    sub = iota((8, 128), 0)
+    which = jnp.zeros((8, 128), I32)
+    for k in range(8):
+        near = chosen_ref[0, block * 8 + k]
+        far = chosen_ref[0, 32 + block * 8 + k]
+        which = jnp.where(sub == k, jnp.where(lane < 64, near, far), which)
+    values = [jnp.zeros((8, 128), F32) for _ in range(16)]
+    for cam in range(16):
+        here = which == cam
+        values = [
+            jnp.where(here, camera_ref[k, cam], value) for k, value in enumerate(values)
+        ]
+    return values
+
+
+def row_index(send_ref, index):
+    index[...] = jnp.concatenate([send_ref[:32, :], send_ref[32:, :]], axis=1)
+
+
+def send_kernel(camera_ref, chosen_ref, send_ref, params_ref, out_ref, raw_ref, table, index, feats):
+    row_index(send_ref, index)
+    for hi in range(8):
+        piece = params_ref[:, 512 * hi : 512 * hi + 512]
+        piece = jnp.concatenate([piece, jnp.zeros((5, 512), F32)], axis=0)
+        high, mid, low = split3(piece)
+        table[144 * hi : 144 * hi + 64, :] = high
+        table[144 * hi + 64 : 144 * hi + 128, :] = mid
+        table[144 * hi + 128 : 144 * hi + 144, :] = low[:16]
+
+    def pick(block, carry):
+        here = jnp.concatenate(
+            [index[pl.ds(2 * block, 1), :], index[pl.ds(2 * block + 1, 1), :]], axis=1
+        )
+        onehot = jnp.where(iota((512, 256), 0) == (here & 511), 1.0, 0.0).astype(BF16)
+        found = dot(table[...], onehot)
+        bank = here >> 9
+        value = jnp.zeros((64, 256), F32)
+        for hi in range(8):
+            high = found[144 * hi : 144 * hi + 64]
+            mid = found[144 * hi + 64 : 144 * hi + 128]
+            low = found[144 * hi + 128 : 144 * hi + 144]
+            mid = jnp.concatenate([mid[:16] + low, mid[16:]], axis=0)
+            value = jnp.where(bank == hi, high + mid, value)
+        raw_ref[pl.ds(2 * block, 64, stride=32), :] = value[:, :128]
+        raw_ref[pl.ds(2 * block + 1, 64, stride=32), :] = value[:, 128:]
+        return carry
+
+    lax.fori_loop(0, 16, pick, 0)
+
+    def shape(block, carry):
+        camera = camera_block(camera_ref, chosen_ref, block)
+        start = pl.multiple_of(block * 8, 8)
+        raw = [raw_ref[pl.ds(32 * p + start, 8), :] for p in range(59)]
+        for feat, value in enumerate(sent_features(raw, camera)):
+            feats[pl.ds(32 * feat + start, 8), :] = value
+        return carry
+
+    lax.fori_loop(0, 4, shape, 0)
+    for half in range(2):
+        lanes = slice(64 * half, 64 * half + 64)
+        for pair in range(5):
+            left = feats[64 * pair : 64 * pair + 32, lanes]
+            if pair < 4:
+                right = feats[64 * pair + 32 : 64 * pair + 64, lanes]
+            else:
+                right = jnp.zeros((32, 64), F32)
+            out_ref[pl.ds(160 * half + pair, 32, stride=5), :] = jnp.concatenate(
+                [left, right], axis=1
+            )
+
+
+def back_kernel(
+    camera_ref, chosen_ref, send_ref, raw_ref, back_ref, first_ref, second_ref,
+    index, feats, grads, spread, onehot,
+):
+    row_index(send_ref, index)
+    for pair in range(5):
+        near = back_ref[pl.ds(pair, 32, stride=5), :]
+        far = back_ref[pl.ds(160 + pair, 32, stride=5), :]
+        feats[64 * pair : 64 * pair + 32, :] = jnp.concatenate([near[:, :64], far[:, :64]], axis=1)
+        feats[64 * pair + 32 : 64 * pair + 64, :] = jnp.concatenate(
+            [near[:, 64:], far[:, 64:]], axis=1
+        )
+    grads[59 * 32 :, :] = jnp.zeros((5 * 32, 128), F32)
+
+    def pull_back(block, carry):
+        camera = camera_block(camera_ref, chosen_ref, block)
+        start = pl.multiple_of(block * 8, 8)
+        raw = [raw_ref[pl.ds(32 * p + start, 8), :] for p in range(59)]
+        _, pull = jax.vjp(lambda rows: sent_features(rows, camera), raw)
+        (found,) = pull([feats[pl.ds(32 * feat + start, 8), :] for feat in range(9)])
+        for p in range(59):
+            grads[pl.ds(32 * p + start, 8), :] = found[p]
+        return carry
+
+    lax.fori_loop(0, 4, pull_back, 0)
+
+    def lay(block, carry):
+        here = index[pl.ds(block, 1), :]
+        lanes = pl.ds(pl.multiple_of(block * 128, 128), 128)
+        onehot[:, lanes] = jnp.where(iota((512, 128), 0) == (here & 511), 1.0, 0.0).astype(BF16)
+        bank = here >> 9
+        high, mid = split2(grads[pl.ds(block, 64, stride=32), :])
+        both = jnp.concatenate([high.astype(F32), mid.astype(F32)], axis=0)
+        for hi in range(8):
+            spread[128 * hi : 128 * hi + 128, lanes] = jnp.where(bank == hi, both, 0.0).astype(BF16)
+        return carry
+
+    lax.fori_loop(0, 32, lay, 0)
+    for hi in range(8):
+        total = dot(spread[128 * hi : 128 * hi + 128, :], onehot[...], NT)
+        total = total[:64] + total[64:]
+        first_ref[:, 512 * hi : 512 * hi + 512] = total[:32]
+        second_ref[:, 512 * hi : 512 * hi + 512] = total[32:]
+
+
+def whole(space):
+    return pl.BlockSpec(memory_space=space)
+
+
+LIMIT = pltpu.CompilerParams(vmem_limit_bytes=56 * 1024 * 1024)
+
+
+def send_rows(cameras, chosen, send, params):
+    return pl.pallas_call(
+        send_kernel,
+        out_shape=(
+            jax.ShapeDtypeStruct((320, 128), F32),
+            jax.ShapeDtypeStruct((2048, 128), F32),
+        ),
+        in_specs=[whole(pltpu.SMEM), whole(pltpu.SMEM), whole(pltpu.VMEM), whole(pltpu.VMEM)],
+        out_specs=(whole(pltpu.VMEM), whole(pltpu.VMEM)),
+        scratch_shapes=[
+            pltpu.VMEM((8 * 144, 512), BF16),
+            pltpu.VMEM((32, 128), I32),
+            pltpu.VMEM((9 * 32, 128), F32),
+        ],
+        compiler_params=LIMIT,
+        name="send_rows",
+    )(cameras, chosen, send, params)
+
+
+def pull_rows(cameras, chosen, send, raw, back):
+    return pl.pallas_call(
+        back_kernel,
+        out_shape=(
+            jax.ShapeDtypeStruct((32, 4096), F32),
+            jax.ShapeDtypeStruct((32, 4096), F32),
+        ),
+        in_specs=[
+            whole(pltpu.SMEM), whole(pltpu.SMEM), whole(pltpu.VMEM), whole(pltpu.VMEM),
+            whole(pltpu.VMEM),
+        ],
+        out_specs=(whole(pltpu.VMEM), whole(pltpu.VMEM)),
+        scratch_shapes=[
+            pltpu.VMEM((32, 128), I32),
+            pltpu.VMEM((10 * 32, 128), F32),
+            pltpu.VMEM((2048, 128), F32),
+            pltpu.VMEM((1024, 4096), BF16),
+            pltpu.VMEM((512, 4096), BF16),
+        ],
+        compiler_params=LIMIT,
+        name="pull_rows",
+    )(cameras, chosen, send, raw, back)
+
+
 def adam_update(params, adam_m, adam_v, gradient):
     rates = jnp.asarray(learn_rates, jnp.float32)[:, None]
     new_m = 0.9 * adam_m + 0.1 * gradient
@@ -407,48 +583,32 @@
     return (new_params, new_m, new_v)
 
 
-def sent_features(raw, camera):
-    feats = project(raw, camera)
-    log2_e = 1.0 / LN2
-    return jnp.stack(
-        [
-            feats[0],
-            feats[1],
-            (-0.5 * log2_e) * feats[2],
-            -log2_e * feats[3],
-            (-0.5 * log2_e) * feats[4],
-            jnp.log(feats[5]) * log2_e,
-            feats[6],
-            feats[7],
-            feats[8],
-        ]
-    )
-
-
 def on_device(
     params, adam_m, adam_v, cameras, device_camera, send_index, slot_rows, tile_ids, target
 ):
-    local = send_index[0, 0].reshape(-1)
-    raw = jnp.take(params, local, axis=1).reshape(-1, 32, 128)
-    dest_cameras = jnp.take(cameras, device_camera[0], axis=1)
-    camera = jnp.repeat(dest_cameras, 64, axis=1).reshape(16, 32, 128)
-    features, pull = jax.vjp(lambda rows: sent_features(rows, camera), raw)
-    outgoing = features.reshape(9, 64, 64).transpose(1, 0, 2).reshape(64, 576)
-    incoming = lax.all_to_all(outgoing, "gs", 0, 0, tiled=True)
+    outgoing, raw = send_rows(cameras, device_camera, send_index[0, 0], params)
+    incoming = lax.all_to_all(outgoing.reshape(64, 1, 640), "gs", 0, 0, tiled=True)
     colours, back = render(
-        jnp.pad(incoming, ((0, 0), (0, 64))),
-        slot_rows[0, 0],
-        tile_ids[0],
-        target[0, 0].transpose(1, 0, 2),
+        incoming.reshape(320, 128), slot_rows[0, 0], tile_ids[0], target[0, 0].transpose(1, 0, 2)
     )
-    returned = lax.all_to_all(back[:, :576], "gs", 0, 0, tiled=True)
-    (raw_grads,) = pull(returned.reshape(64, 9, 64).transpose(1, 0, 2).reshape(9, 32, 128))
-    gradient = jax.ops.segment_sum(
-        raw_grads.reshape(59, -1).T, local, num_segments=params.shape[1]
-    ).T
-    total = lax.psum(gradient, "img")
+    returned = lax.all_to_all(back.reshape(64, 1, 640), "gs", 0, 0, tiled=True)
+    first, second = pull_rows(
+        cameras, device_camera, send_index[0, 0], raw, returned.reshape(320, 128)
+    )
+    first, second = total_over_images(first, second)
+    total = jnp.concatenate([first, second], axis=0)[:59]
     new_params, new_m, new_v = adam_update(params, adam_m, adam_v, total)
     return (new_params, new_m, new_v, colours.transpose(1, 0, 2)[None, None])
+
+
+def total_over_images(first, second):
+    near = [(i, i ^ 1) for i in range(4)]
+    far = [(i, 3 - i) for i in range(4)]
+    first, second = (
+        first + lax.ppermute(first, "img", near),
+        second + lax.ppermute(second, "img", far),
+    )
+    return first + lax.ppermute(first, "img", far), second + lax.ppermute(second, "img", near)
 
 
 def solution(mesh):

time: 200 us -> 134 us (0.67)
  local copies, waits for them, and re-layouts: 40.2 us -> 2.15 us
  other arithmetic: 35.3 us -> 3.35 us
  Pallas kernels: 29.9 us -> 59.8 us
  waiting for transfers between devices: 60.6 us -> 31.8 us
  blocking collectives: 0 us -> 16.1 us
  between operations: 15 us -> 0.7 us
    psum x1 -> x0, waiting for transfers between devices: 48 us -> none  [on_device(): total = lax.psum(gradient, 'img')]
    pallas_call x0 -> x2, Pallas kernels: none -> 29.8 us  [the longest x1 18.7 us: pull_rows(): pl.pallas_call(back_kernel, out_shape=(jax.ShapeDtypeStruct((32, 4096), F...]
    scatter-add x1 -> x0, other arithmetic: 23.2 us -> none  [on_device(): jax.ops.segment_sum(raw_grads.reshape(59, -1).T, local, num_segments=para...]
    ppermute x0 -> x4, waiting for transfers between devices: none -> 23.1 us  [the longest x1 11.2 us: total_over_images(): lax.ppermute(first, 'img', far)]
    gather x3 -> x0, local copies, waits for them, and re-layouts: 16.9 us -> none  [the longest x2 16.3 us: on_device(): raw = jnp.take(params, local, axis=1).reshape(-1, 32, 128)]
    all_to_all x0 -> x1, blocking collectives: none -> 16.1 us  [on_device(): returned = lax.all_to_all(back.reshape(64, 1, 640), 'gs', 0, 0, tiled=True)]
    ppermute x0 -> x4, starting transfers between devices: none -> 6.72 us  [the longest x1 2.84 us: total_over_images(): lax.ppermute(first, 'img', far)]
    all_to_all x2 -> x1, starting transfers between devices: 18.3 us -> 12.2 us  [on_device(): lax.all_to_all(outgoing.reshape(64, 1, 640), 'gs', 0, 0, tiled=True)]
  transfers between devices with their start and end apart: 3 -> 5, of which waited for: 3 -> 4; matrix products, arithmetic and copies ran while one was open for 3% -> 2% of each run, Pallas kernels for 0% -> 0%
where the time goes in v2:
time: 134 us; the launch traced here: 133 us
  Pallas kernels  59.8 us (45%)
  waiting for transfers between devices  31.8 us (24%)
  starting transfers between devices  19 us (14%)
  blocking collectives  16.1 us (12%)
  other arithmetic  3.35 us (2%)
  local copies, waits for them, and re-layouts  2.15 us (2%)
    pallas_call x1, Pallas kernels, render(): pl.pallas_call(render_kernel, out_shape=(jax.ShapeDtypeStruct((3, tiles,...  29.9 us
    pallas_call x1, Pallas kernels, pull_rows(): pl.pallas_call(back_kernel, out_shape=(jax.ShapeDtypeStruct((32, 4096), F...  18.7 us
    all_to_all x1, blocking collectives, on_device(): returned = lax.all_to_all(back.reshape(64, 1, 640), 'gs', 0, 0, tiled=True)  16.1 us
    all_to_all x1, starting transfers between devices, on_device(): lax.all_to_all(outgoing.reshape(64, 1, 640), 'gs', 0, 0, tiled=True)  12.2 us
    ppermute x1, waiting for transfers between devices, total_over_images(): lax.ppermute(first, 'img', far)  11.2 us
    pallas_call x1, Pallas kernels, send_rows(): pl.pallas_call(send_kernel, out_shape=(jax.ShapeDtypeStruct((320, 128), F...  11.1 us
    ppermute x1, waiting for transfers between devices, total_over_images(): lax.ppermute(first, 'img', near)  10.6 us
    all_to_all x1, waiting for transfers between devices, on_device(): lax.all_to_all(outgoing.reshape(64, 1, 640), 'gs', 0, 0, tiled=True)  8.63 us
  transfers between devices with their start and end apart: 5, of which 4 were waited for; matrix products, arithmetic and copies ran while one was open for 2% of the time, Pallas kernels for 0%

profile of v2, /device:TPU:8, one launch (start us, length us, event | category | flops | bytes accessed | tf_op | source)
XLA Modules:
  0.0 132.7 jit_solution(3779306938534316278)
XLA Ops:
  0.6 11.1 %send_rows.1 = (f32[320,128]{1,0:T(8,128)}, f32[2048,128]{1,0:T(8,128)}) custom-call(f32[16,16]{1,0:T(8,128)} %camera_ref.3, s32[1,64]{1,0:T(1,128)} %chosen_ref.3, s32[64,64]{1,0:T(8,128)} %bitcast.19, f32[59,4096]{1,0:T(8,128)} %params_ref.1), custom_call_target="tpu_custom_call" | custom-call | tf_op jit(solution)/shard_map/send_rows/pallas_call | solution.py:536
  11.7 0.0 copy-start.5
  11.7 12.2 %all-to-all-start = ((f32[64,1,640]{2,1,0:T(1,128)}), f32[64,1,640]{2,1,0:T(1,128)S(1)}, u32[]{:S(2)}, u32[]{:S(2)}) async-start(f32[64,1,640]{2,1,0:T(1,128)} %bitcast.17), calls=%async_computation | async-start | bytes 327680 | tf_op jit(solution)/shard_map/all_to_all | solution.py:590
  24.0 0.0 copy-done.5
  24.0 0.2 copy.18
  24.2 0.9 reshape.29.slots_ref
  25.1 8.6 %all-to-all-done = f32[64,1,640]{2,1,0:T(1,128)S(1)} async-done(((f32[64,1,640]{2,1,0:T(1,128)}), f32[64,1,640]{2,1,0:T(1,128)S(1)}, u32[]{:S(2)}, u32[]{:S(2)}) %all-to-all-start) | async-done | bytes 163872 | tf_op jit(solution)/shard_map/all_to_all | solution.py:590
  33.7 0.0 copy-start.3
  33.7 0.7 copy-done.3
  34.4 29.9 %render.1 = (f32[3,32,256]{2,1,0:T(8,128)}, f32[320,128]{1,0:T(8,128)}) custom-call(s32[1,32]{1,0:T(1,128)} %bitcast.23, f32[320,128]{1,0:T(8,128)} %bitcast.16, s32[4,1,2048]{2,1,0:T(1,128)} %reshape.29.slots_ref, f32[3,32,256]{2,1,0:T(8,128)} %bitcast.21), custom_call_target="tpu_custom_call" | custom-call | tf_op jit(solution)/shard_map/render/pallas_call | solution.py:371
  64.3 16.1 %all_to_all.10 = f32[64,1,640]{2,1,0:T(1,128)} all-to-all(f32[64,1,640]{2,1,0:T(1,128)} %bitcast.18), channel_id=1, replica_groups=mesh['img'=4,'gs'=64] {'gs'}, dimensions={0} | all-to-all | bytes 327680 | tf_op jit(solution)/shard_map/all_to_all | solution.py:594
  80.4 18.7 %pull_rows.1 = (f32[32,4096]{1,0:T(8,128)}, f32[32,4096]{1,0:T(8,128)}) custom-call(f32[16,16]{1,0:T(8,128)} %camera_ref.3, s32[1,64]{1,0:T(1,128)} %chosen_ref.3, s32[64,64]{1,0:T(8,128)} %bitcast.20, f32[2048,128]{1,0:T(8,128)} %get-tuple-element.10.raw_ref, f32[320,128]{1,0:T(8,128)} %bitcast.15), custom_call_target="tpu_custom_call" | custom-call | tf_op jit(solution)/shard_map/pull_rows/pallas_call | solution.py:555
  99.1 1.5 %collective-permute-start = (f32[32,4096]{1,0:T(8,128)}, f32[32,4096]{1,0:T(8,128)S(1)}, u32[]{:S(2)}, u32[]{:S(2)}) collective-permute-start(f32[32,4096]{1,0:T(8,128)} %get-tuple-element.13), channel_id=1, source_target_pairs={{0,64},{64,0},{128,192},{192,128},{1,65},{65,1},{129,193},{193,129... | collective-permute-start | bytes 1572872 | tf_op jit(solution)/shard_map/ppermute | solution.py:608
  100.6 0.0 copy-start.4
  100.6 2.1 %collective-permute-start.2 = (f32[32,4096]{1,0:T(8,128)}, f32[32,4096]{1,0:T(8,128)S(1)}, u32[]{:S(2)}, u32[]{:S(2)}) collective-permute-start(f32[32,4096]{1,0:T(8,128)} %get-tuple-element.14), channel_id=1, source_target_pairs={{0,192},{64,128},{128,64},{192,0},{1,193},{65,129},{129,65},{193,1... | collective-permute-start | bytes 1572872 | tf_op jit(solution)/shard_map/ppermute | solution.py:609
  102.7 10.6 %collective-permute-done = f32[32,4096]{1,0:T(8,128)S(1)} collective-permute-done((f32[32,4096]{1,0:T(8,128)}, f32[32,4096]{1,0:T(8,128)S(1)}, u32[]{:S(2)}, u32[]{:S(2)}) %collective-permute-start) | collective-permute-done | bytes 524320 | tf_op jit(solution)/shard_map/ppermute | solution.py:608
  113.3 1.1 add.24
  114.4 2.8 %collective-permute-start.1 = (f32[32,4096]{1,0:T(8,128)S(1)}, f32[32,4096]{1,0:T(8,128)S(1)}, u32[]{:S(2)}, u32[]{:S(2)}) collective-permute-start(f32[32,4096]{1,0:T(8,128)S(1)} %add.24), channel_id=1, source_target_pairs={{0,192},{64,128},{128,64},{192,0},{1,193},{65,129},{129,65},{193,1... | collective-permute-start | bytes 1572872 | tf_op jit(solution)/shard_map/ppermute | solution.py:611
  117.2 0.0 collective-permute-done.2
  117.2 0.0 copy-done.4
  117.2 0.0 copy-start.6
  117.2 0.1 add.26
  117.3 0.3 collective-permute-start.3
  117.6 11.2 %collective-permute-done.1 = f32[32,4096]{1,0:T(8,128)S(1)} collective-permute-done((f32[32,4096]{1,0:T(8,128)S(1)}, f32[32,4096]{1,0:T(8,128)S(1)}, u32[]{:S(2)}, u32[]{:S(2)}) %collective-permute-start.1) | collective-permute-done | bytes 524320 | tf_op jit(solution)/shard_map/ppermute | solution.py:611
  128.8 0.0 copy-start.1
  128.8 0.0 copy-start.2
  128.8 0.1 add.25
  128.8 0.0 copy-start
  128.9 1.3 %collective-permute-done.3 = f32[32,4096]{1,0:T(8,128)S(1)} collective-permute-done((f32[32,4096]{1,0:T(8,128)S(1)}, f32[32,4096]{1,0:T(8,128)S(1)}, u32[]{:S(2)}, u32[]{:S(2)}) %collective-permute-start.3) | collective-permute-done | bytes 524320 | tf_op jit(solution)/shard_map/ppermute | solution.py:611
  130.2 0.1 add.27
  130.3 0.0 copy-done.6
  130.3 0.0 copy-done.1
  130.3 0.0 copy-done.2
  130.3 0.3 copy-done
  130.7 2.1 %divide_subtract_fusion = (f32[59,4096]{1,0:T(8,128)}, f32[59,4096]{1,0:T(8,128)}, f32[59,4096]{1,0:T(8,128)}) fusion(f32[59,4096]{1,0:T(8,128)S(1)} %copy-done, f32[59]{0:T(128)S(1)} %copy-done.6, f32[32,4096]{1,0:T(8,128)S(1)} %add.27, f32[32,4096]{1,0:T(8,128)S(1)} %add.25, f32[59,4096]{1,0:T(8,128)S(1)} %copy-done.1, f32[59,4096]{1,0:T(8,128)S(1)} %copy-done.2), kind=kLoop, calls=%fused_computation.3 | loop fusion | flops 3141632 | bytes 6848748 | tf_op jit(solution)/shard_map/sub | solution.py:582
Async XLA Ops:
  11.7 12.2 %copy-start.5 = (s32[1,1,32,256]{3,2,1,0:T(8,128)S(1)}, s32[1,1,32,256]{3,2,1,0:T(8,128)}, u32[]{:S(2)}) copy-start(s32[1,1,32,256]{3,2,1,0:T(8,128)} %param.16) | copy-start | bytes 98308
  11.7 22.0 %all-to-all-start = ((f32[64,1,640]{2,1,0:T(1,128)}), f32[64,1,640]{2,1,0:T(1,128)S(1)}, u32[]{:S(2)}, u32[]{:S(2)}) async-start(f32[64,1,640]{2,1,0:T(1,128)} %bitcast.17), calls=%async_computation | async-start | bytes 327680 | tf_op jit(solution)/shard_map/all_to_all | solution.py:590
  33.7 0.7 copy-start.3
  99.1 14.2 %collective-permute-start = (f32[32,4096]{1,0:T(8,128)}, f32[32,4096]{1,0:T(8,128)S(1)}, u32[]{:S(2)}, u32[]{:S(2)}) collective-permute-start(f32[32,4096]{1,0:T(8,128)} %get-tuple-element.13), channel_id=1, source_target_pairs={{0,64},{64,0},{128,192},{192,128},{1,65},{65,1},{129,193},{193,129... | collective-permute-start | bytes 1572872 | tf_op jit(solution)/shard_map/ppermute | solution.py:608
  100.6 16.7 %copy-start.4 = (f32[32,4096]{1,0:T(8,128)S(1)}, f32[32,4096]{1,0:T(8,128)}, u32[]{:S(2)}) copy-start(f32[32,4096]{1,0:T(8,128)} %get-tuple-element.14) | copy-start | bytes 1572868
  100.6 16.7 %collective-permute-start.2 = (f32[32,4096]{1,0:T(8,128)}, f32[32,4096]{1,0:T(8,128)S(1)}, u32[]{:S(2)}, u32[]{:S(2)}) collective-permute-start(f32[32,4096]{1,0:T(8,128)} %get-tuple-element.14), channel_id=1, source_target_pairs={{0,192},{64,128},{128,64},{192,0},{1,193},{65,129},{129,65},{193,1... | collective-permute-start | bytes 1572872 | tf_op jit(solution)/shard_map/ppermute | solution.py:609
  114.4 14.4 %collective-permute-start.1 = (f32[32,4096]{1,0:T(8,128)S(1)}, f32[32,4096]{1,0:T(8,128)S(1)}, u32[]{:S(2)}, u32[]{:S(2)}) collective-permute-start(f32[32,4096]{1,0:T(8,128)S(1)} %add.24), channel_id=1, source_target_pairs={{0,192},{64,128},{128,64},{192,0},{1,193},{65,129},{129,65},{193,1... | collective-permute-start | bytes 1572872 | tf_op jit(solution)/shard_map/ppermute | solution.py:611
  117.2 13.0 %copy-start.6 = (f32[59]{0:T(128)S(1)}, f32[59]{0:T(128)}, u32[]{:S(2)}) copy-start(f32[59]{0:T(128)} %constant.24) | copy-start | bytes 712
  117.3 12.9 %collective-permute-start.3 = (f32[32,4096]{1,0:T(8,128)S(1)}, f32[32,4096]{1,0:T(8,128)S(1)}, u32[]{:S(2)}, u32[]{:S(2)}) collective-permute-start(f32[32,4096]{1,0:T(8,128)S(1)} %add.26), channel_id=1, source_target_pairs={{0,64},{64,0},{128,192},{192,128},{1,65},{65,1},{129,193},{193,129... | collective-permute-start | bytes 1572872 | tf_op jit(solution)/shard_map/ppermute | solution.py:611
  128.8 1.5 %copy-start.1 = (f32[59,4096]{1,0:T(8,128)S(1)}, f32[59,4096]{1,0:T(8,128)}, u32[]{:S(2)}) copy-start(f32[59,4096]{1,0:T(8,128)} %param.11) | copy-start | bytes 2899972
  128.8 1.5 %copy-start.2 = (f32[59,4096]{1,0:T(8,128)S(1)}, f32[59,4096]{1,0:T(8,128)}, u32[]{:S(2)}) copy-start(f32[59,4096]{1,0:T(8,128)} %param.12) | copy-start | bytes 2899972
  128.8 1.8 %copy-start = (f32[59,4096]{1,0:T(8,128)S(1)}, f32[59,4096]{1,0:T(8,128)}, u32[]{:S(2)}) copy-start(f32[59,4096]{1,0:T(8,128)} %params_ref.1) | copy-start | bytes 2899972

commit v3 on v2

--- a/solution.py
+++ b/solution.py
@@ -177,13 +177,22 @@
     return lax.broadcasted_iota(I32, shape, dim)
 
 
+def wide(tinted, at, ch):
+    value = tinted[at, 128 * ch : 128 * ch + 128]
+    return jnp.concatenate([value, value], axis=1)
+
+
 def render_kernel(
     tid_ref, recv_ref, slots_ref, target_ref, colour_ref, out_ref,
-    table, onehot, coef, power_w, diff_w, alpha, weight, weight_h, weight_l, pull,
-    dp_h, dp_m, dp_l, spread, total, mono,
+    table, onehot, coef, power_w, turned, alpha, weight, weight_h, weight_l, pixel_w,
+    spread, total, tint_w, tinted,
 ):
     groups, _, rows = slots_ref.shape
-    slots = rows // 8
+    many = target_ref.shape[1] // groups
+    tints = 3 * many
+    edge = 16 + 2 * tints
+    chunks = rows // 256
+    depth = coef.shape[0]
     for feat in range(9):
         side = slice(64 * (feat % 2), 64 * (feat % 2) + 64)
         block = jnp.concatenate(
@@ -194,11 +203,6 @@
             table[pl.ds((part * 9 + feat) * 16, 16), :] = piece
     total[...] = jnp.zeros_like(total)
     coef[...] = jnp.zeros_like(coef)
-    diff_w[...] = jnp.zeros_like(diff_w)
-    pixel = iota((16, 256), 1)
-    off_u = (pixel & 15).astype(F32) - 7.5
-    off_v = (pixel >> 4).astype(F32) - 7.5
-    which = iota((16, 256), 0)
     def pick(kind, u, v):
         out = jnp.where(kind == 0, 1.0, 0.0)
         out = jnp.where(kind == 1, u, out)
@@ -206,9 +210,14 @@
         out = jnp.where(kind == 3, u * u, out)
         out = jnp.where(kind == 4, u * v, out)
         return jnp.where(kind == 5, v * v, out)
-    mono[...] = pick(which, off_u, off_v).astype(BF16)
-    row = iota((128, 256), 0)
-    pix = iota((128, 256), 1)
+    pix = iota((256, 128), 0)
+    mono = pick(
+        iota((256, 128), 1), (pix & 15).astype(F32) - 7.5, (pix >> 4).astype(F32) - 7.5
+    ).astype(BF16)
+    pixel_w[:256, :] = mono
+    pixel_w[256:512, :] = mono
+    row = iota((depth, 256), 0)
+    pix = iota((depth, 256), 1)
     kind = jnp.where(row >= 12, row - 12, jnp.where(row >= 6, row - 6, row))
     power_w[...] = jnp.where(
         row < 18,
@@ -216,8 +225,12 @@
         0.0,
     ).astype(BF16)
 
-    lane_tile = iota((1, rows), 1) & 7
-    own = iota((8, rows), 0) == lane_tile
+    row = iota((depth, 384), 0)
+    first_row = 18 + 3 * (iota((depth, 384), 1) >> 7)
+    tint_w[...] = jnp.where((row >= first_row) & (row < first_row + 3), 1.0, 0.0).astype(BF16)
+
+    lane_tile = iota((1, rows), 1) & (many - 1)
+    own = iota((many, rows), 0) == lane_tile
     hi_row = iota((16, rows), 0)
 
     def group(step, carry):
@@ -237,8 +250,8 @@
         mean_x, mean_y, con_a, con_b, con_c, log_op = feats[:6]
         centre_x = jnp.zeros((1, rows), F32)
         centre_y = jnp.zeros((1, rows), F32)
-        for t in range(8):
-            tid = tid_ref[0, step * 8 + t]
+        for t in range(many):
+            tid = tid_ref[0, step * many + t]
             centre_x = jnp.where(lane_tile == t, ((tid & 15) * 16 + 8).astype(F32), centre_x)
             centre_y = jnp.where(lane_tile == t, ((tid >> 4) * 16 + 8).astype(F32), centre_y)
         far_x = centre_x - mean_x
@@ -255,75 +268,66 @@
             for part, piece in enumerate(split3(value)):
                 coef[pl.ds(part * 6 + m, 1), :] = piece.astype(F32)
         for ch in range(3):
-            c_high, c_mid = split2(feats[6 + ch])
-            c_high = jnp.where(own, c_high.astype(F32), 0.0)
-            coef[24 + 8 * ch : 32 + 8 * ch, :] = c_high
-            coef[48 + 8 * ch : 56 + 8 * ch, :] = jnp.where(own, c_mid.astype(F32), 0.0)
-            coef[72 + 8 * ch : 80 + 8 * ch, :] = c_high
-        turned = jnp.transpose(coef[...]).astype(BF16)
-        alpha[...] = dot(turned, power_w[...])
-
-        def forward(chunk, passed):
-            base = pl.multiple_of(chunk * 128, 128)
-            powers = alpha[pl.ds(base, 128), :]
-            alphas = jnp.exp2(powers)
-            alpha[pl.ds(base, 128), :] = alphas
+            for part, piece in enumerate(split3(feats[6 + ch])):
+                coef[pl.ds(18 + 3 * ch + part, 1), :] = piece.astype(F32)
+        turned[...] = jnp.transpose(coef[...]).astype(BF16)
+
+        passed = jnp.ones((many, 256), F32)
+        shown = [jnp.zeros((many, 256), F32)] * 3
+        for chunk in range(chunks):
+            part = slice(256 * chunk, 256 * chunk + 256)
+            alphas = jnp.exp2(dot(turned[part, :], power_w[...]))
+            tinted[part, :] = dot(turned[part, :], tint_w[...])
+            alpha[part, :] = alphas
             out = []
-            for k in range(16):
-                w = passed * alphas[8 * k : 8 * k + 8]
+            for k in range(0, 256, many):
+                w = passed * alphas[k : k + many]
                 passed = passed - w
+                at = slice(256 * chunk + k, 256 * chunk + k + many)
+                shown = [value + w * wide(tinted, at, ch) for ch, value in enumerate(shown)]
                 out.append(w)
             out = jnp.concatenate(out, axis=0)
-            weight[pl.ds(base, 128), :] = out
+            weight[part, :] = out
             w_h, w_l = split2(out)
-            weight_h[pl.ds(base, 128), :] = w_h
-            weight_l[pl.ds(base, 128), :] = w_l
-            return passed
-
-        lax.fori_loop(0, slots // 16, forward, jnp.ones((8, 256), F32))
-        tinted = coef[24:72, :].astype(BF16)
-        first = dot(tinted, weight_h[...])
-        second = dot(tinted, weight_l[...])
-        shown = first[:24] + (first[24:48] + second[:24])
-        diffs_h, diffs_m = [], []
+            weight_h[part, :] = w_h
+            weight_l[part, :] = w_l
+        diffs = []
         for ch in range(3):
-            colour = shown[8 * ch : 8 * ch + 8]
-            where = pl.ds(pl.multiple_of(step * 8, 8), 8)
-            colour_ref[ch, where, :] = colour
-            d_high, d_mid = split2(colour - target_ref[ch, where, :])
-            d_high = d_high.astype(F32)
-            diffs_h.append(d_high)
-            diffs_m.append(d_mid.astype(F32))
-            diff_w[24 + 8 * ch : 32 + 8 * ch, :] = d_high
-            diff_w[48 + 8 * ch : 56 + 8 * ch, :] = d_high
-            diff_w[72 + 8 * ch : 80 + 8 * ch, :] = d_mid.astype(F32)
-        pull[...] = dot(turned, diff_w[...].astype(BF16))
-
-        def backward(chunk, behind):
-            base = pl.multiple_of((slots // 16 - 1 - chunk) * 128, 128)
-            alphas = alpha[pl.ds(base, 128), :]
-            weights = weight[pl.ds(base, 128), :]
-            pulls = pull[pl.ds(base, 128), :]
-            out = [None] * 16
-            for k in range(15, -1, -1):
-                gap = pulls[8 * k : 8 * k + 8] - behind
-                out[k] = weights[8 * k : 8 * k + 8] * gap
-                behind = behind + alphas[8 * k : 8 * k + 8] * gap
-            out = jnp.concatenate(out, axis=0)
-            d_h, d_m, d_l = split3(out)
-            dp_h[pl.ds(base, 128), :] = d_h
-            dp_m[pl.ds(base, 128), :] = d_m
-            dp_l[pl.ds(base, 128), :] = d_l
-            return behind
-
-        lax.fori_loop(0, slots // 16, backward, jnp.zeros((8, 256), F32))
-        diff48 = diff_w[48:96, :].astype(BF16)
-        tint_h = dot(diff48, weight_h[...], NT)
-        tint_l = dot(diff48, weight_l[...], NT)
-        tint = tint_h[:24] + (tint_h[24:48] + tint_l[:24])
-        moments = (
-            dot(mono[...], dp_l[...], NT) + dot(mono[...], dp_m[...], NT)
-        ) + dot(mono[...], dp_h[...], NT)
+            where = pl.ds(pl.multiple_of(step * many, many), many)
+            colour_ref[ch, where, :] = shown[ch]
+            diffs.append(shown[ch] - target_ref[ch, where, :])
+        d_high = [value.astype(BF16).astype(F32) for value in diffs]
+        d_mid = [value - high for value, high in zip(diffs, d_high)]
+        front = jnp.zeros((16, 256), F32)
+        back = jnp.zeros((128 - edge, 256), F32)
+        pixel_w[512:768, :] = jnp.transpose(
+            jnp.concatenate([front] + d_high + d_mid + [back], axis=0)
+        ).astype(BF16)
+        pixel_w[768:, :] = jnp.transpose(
+            jnp.concatenate([front] + d_high + [jnp.zeros((112 - tints, 256), F32)], axis=0)
+        ).astype(BF16)
+
+        behind = jnp.zeros((many, 256), F32)
+        sums = [None] * chunks
+        for chunk in range(chunks - 1, -1, -1):
+            part = slice(256 * chunk, 256 * chunk + 256)
+            alphas = alpha[part, :]
+            weights = weight[part, :]
+            out = []
+            for k in range(256 - many, -1, -many):
+                at = slice(256 * chunk + k, 256 * chunk + k + many)
+                pulls = (
+                    diffs[0] * wide(tinted, at, 0) + diffs[1] * wide(tinted, at, 1)
+                ) + diffs[2] * wide(tinted, at, 2)
+                gap = pulls - behind
+                out.append(weights[k : k + many] * gap)
+                behind = behind + alphas[k : k + many] * gap
+            d_h, d_l = split2(jnp.concatenate(out[::-1], axis=0))
+            both = jnp.concatenate([d_h, d_l, weight_h[part, :], weight_l[part, :]], axis=1)
+            sums[chunk] = jnp.transpose(dot(both, pixel_w[...]))
+        sums = jnp.concatenate(sums, axis=1)
+        moments = sums[:16]
+        tint = sums[16 : 16 + tints] + sums[16 + tints : edge]
         s_0, s_u, s_v, s_uu, s_uv, s_vv = [LN2 * moments[m : m + 1] for m in range(6)]
         sum_x = far_x * s_0 + s_u
         sum_y = far_y * s_0 + s_v
@@ -335,11 +339,13 @@
             far_y * (sum_y + s_v) + s_vv,
             s_0,
         ] + [
-            jnp.sum(jnp.where(own, tint[8 * ch : 8 * ch + 8], 0.0), axis=0, keepdims=True)
+            jnp.sum(
+                jnp.where(own, tint[many * ch : many * ch + many], 0.0), axis=0, keepdims=True
+            )
             for ch in range(3)
         ]
         for feat in range(9):
-            for part, piece in enumerate(split3(grads[feat])):
+            for part, piece in enumerate(split2(grads[feat])):
                 spread[pl.ds((part * 9 + feat) * 16, 16), :] = jnp.where(
                     mask, piece.astype(F32), 0.0
                 ).astype(BF16)
@@ -349,10 +355,7 @@
     lax.fori_loop(0, groups, group, 0)
     grids = []
     for feat in range(9):
-        grids.append(
-            (total[16 * feat + 288 : 16 * feat + 304] + total[16 * feat + 144 : 16 * feat + 160])
-            + total[16 * feat : 16 * feat + 16]
-        )
+        grids.append(total[16 * feat + 144 : 16 * feat + 160] + total[16 * feat : 16 * feat + 16])
     grids.append(jnp.zeros((16, 256), F32))
     for pair in range(5):
         for j in range(4):
@@ -362,47 +365,37 @@
             )
 
 
-def render(recv, slot_rows, tile_ids, target):
+def render(recv, slot_rows, tile_ids, target, many=16):
     tiles, slots = slot_rows.shape
-    groups = tiles // 8
-    rows = slots * 8
-    ordered = slot_rows.reshape(groups, 8, slots).transpose(0, 2, 1).reshape(groups, 1, rows)
-    vm = lambda *shape_type: pltpu.VMEM(*shape_type)
+    groups = tiles // many
+    rows = slots * many
+    depth = 32
+    ordered = slot_rows.reshape(groups, many, slots).transpose(0, 2, 1).reshape(groups, 1, rows)
     return pl.pallas_call(
         render_kernel,
         out_shape=(
             jax.ShapeDtypeStruct((3, tiles, 256), F32),
             jax.ShapeDtypeStruct((320, 128), F32),
         ),
-        in_specs=[
-            pl.BlockSpec(memory_space=pltpu.SMEM),
-            pl.BlockSpec(memory_space=pltpu.VMEM),
-            pl.BlockSpec(memory_space=pltpu.VMEM),
-            pl.BlockSpec(memory_space=pltpu.VMEM),
+        in_specs=[whole(pltpu.SMEM)] + [whole(pltpu.VMEM)] * 3,
+        out_specs=(whole(pltpu.VMEM), whole(pltpu.VMEM)),
+        scratch_shapes=[
+            pltpu.VMEM((432, 256), BF16),
+            pltpu.VMEM((256, rows), BF16),
+            pltpu.VMEM((depth, rows), F32),
+            pltpu.VMEM((depth, 256), BF16),
+            pltpu.VMEM((rows, depth), BF16),
+            pltpu.VMEM((rows, 256), F32),
+            pltpu.VMEM((rows, 256), F32),
+            pltpu.VMEM((rows, 256), BF16),
+            pltpu.VMEM((rows, 256), BF16),
+            pltpu.VMEM((1024, 128), BF16),
+            pltpu.VMEM((288, rows), BF16),
+            pltpu.VMEM((288, 256), F32),
+            pltpu.VMEM((depth, 384), BF16),
+            pltpu.VMEM((rows, 384), F32),
         ],
-        out_specs=(
-            pl.BlockSpec(memory_space=pltpu.VMEM),
-            pl.BlockSpec(memory_space=pltpu.VMEM),
-        ),
-        scratch_shapes=[
-            vm((432, 256), BF16),
-            vm((256, rows), BF16),
-            vm((128, rows), F32),
-            vm((128, 256), BF16),
-            vm((128, 256), F32),
-            vm((rows, 256), F32),
-            vm((rows, 256), F32),
-            vm((rows, 256), BF16),
-            vm((rows, 256), BF16),
-            vm((rows, 256), F32),
-            vm((rows, 256), BF16),
-            vm((rows, 256), BF16),
-            vm((rows, 256), BF16),
-            vm((432, rows), BF16),
-            vm((432, 256), F32),
-            vm((16, 256), BF16),
-        ],
-        compiler_params=pltpu.CompilerParams(vmem_limit_bytes=56 * 1024 * 1024),
+        compiler_params=LIMIT,
         name="render",
     )(tile_ids, recv, ordered, target)
 
@@ -438,7 +431,7 @@
         table[144 * hi + 64 : 144 * hi + 128, :] = mid
         table[144 * hi + 128 : 144 * hi + 144, :] = low[:16]
 
-    def pick(block, carry):
+    def pick(block):
         here = jnp.concatenate(
             [index[pl.ds(2 * block, 1), :], index[pl.ds(2 * block + 1, 1), :]], axis=1
         )
@@ -454,9 +447,9 @@
             value = jnp.where(bank == hi, high + mid, value)
         raw_ref[pl.ds(2 * block, 64, stride=32), :] = value[:, :128]
         raw_ref[pl.ds(2 * block + 1, 64, stride=32), :] = value[:, 128:]
-        return carry
-
-    lax.fori_loop(0, 16, pick, 0)
+
+    for block in range(16):
+        pick(block)
 
     def shape(block, carry):
         camera = camera_block(camera_ref, chosen_ref, block)
@@ -506,21 +499,25 @@
 
     lax.fori_loop(0, 4, pull_back, 0)
 
-    def lay(block, carry):
+    def lay(block):
         here = index[pl.ds(block, 1), :]
-        lanes = pl.ds(pl.multiple_of(block * 128, 128), 128)
+        lanes = slice(128 * block, 128 * block + 128)
         onehot[:, lanes] = jnp.where(iota((512, 128), 0) == (here & 511), 1.0, 0.0).astype(BF16)
         bank = here >> 9
         high, mid = split2(grads[pl.ds(block, 64, stride=32), :])
-        both = jnp.concatenate([high.astype(F32), mid.astype(F32)], axis=0)
+        both = jnp.concatenate([high, mid], axis=0)
         for hi in range(8):
-            spread[128 * hi : 128 * hi + 128, lanes] = jnp.where(bank == hi, both, 0.0).astype(BF16)
-        return carry
-
-    lax.fori_loop(0, 32, lay, 0)
+            chosen = jnp.where(bank == hi, 1.0, 0.0).astype(BF16)
+            spread[128 * hi : 128 * hi + 128, lanes] = both * chosen
+
+    everything = jnp.zeros((1024, 512), F32)
+    for part in range(4):
+        for block in range(8 * part, 8 * part + 8):
+            lay(block)
+        lanes = slice(1024 * part, 1024 * part + 1024)
+        everything = everything + dot(spread[:, lanes], onehot[:, lanes], NT)
     for hi in range(8):
-        total = dot(spread[128 * hi : 128 * hi + 128, :], onehot[...], NT)
-        total = total[:64] + total[64:]
+        total = everything[128 * hi : 128 * hi + 64] + everything[128 * hi + 64 : 128 * hi + 128]
         first_ref[:, 512 * hi : 512 * hi + 512] = total[:32]
         second_ref[:, 512 * hi : 512 * hi + 512] = total[32:]
 

time: 134 us -> 112 us (0.84)
  Pallas kernels: 59.8 us -> 37.4 us
    pallas_call x1, Pallas kernels: 18.7 us -> 8.41 us  [pull_rows(): pl.pallas_call(back_kernel, out_shape=(jax.ShapeDtypeStruct((32, 4096), F...]
    pallas_call x1, Pallas kernels: 29.9 us -> 20.5 us  [render(): pl.pallas_call(render_kernel, out_shape=(jax.ShapeDtypeStruct((3, tiles,...]
    pallas_call x1, Pallas kernels: 11.1 us -> 8.47 us  [send_rows(): pl.pallas_call(send_kernel, out_shape=(jax.ShapeDtypeStruct((320, 128), F...]
where the time goes in v3:
time: 112 us; the launch traced here: 110 us
  Pallas kernels  37.4 us (33%)
  waiting for transfers between devices  31.9 us (28%)
  starting transfers between devices  19 us (17%)
  blocking collectives  16 us (14%)
  other arithmetic  3.35 us (3%)
  local copies, waits for them, and re-layouts  1.95 us (2%)
    pallas_call x1, Pallas kernels, render(): pl.pallas_call(render_kernel, out_shape=(jax.ShapeDtypeStruct((3, tiles,...  20.5 us
    all_to_all x1, blocking collectives, on_device(): returned = lax.all_to_all(back.reshape(64, 1, 640), 'gs', 0, 0, tiled=True)  16 us
    all_to_all x1, starting transfers between devices, on_device(): lax.all_to_all(outgoing.reshape(64, 1, 640), 'gs', 0, 0, tiled=True)  12.3 us
    ppermute x1, waiting for transfers between devices, total_over_images(): lax.ppermute(first, 'img', far)  11.2 us
    ppermute x1, waiting for transfers between devices, total_over_images(): lax.ppermute(first, 'img', near)  10.6 us
    all_to_all x1, waiting for transfers between devices, on_device(): lax.all_to_all(outgoing.reshape(64, 1, 640), 'gs', 0, 0, tiled=True)  8.83 us
    pallas_call x1, Pallas kernels, send_rows(): pl.pallas_call(send_kernel, out_shape=(jax.ShapeDtypeStruct((320, 128), F...  8.47 us
    pallas_call x1, Pallas kernels, pull_rows(): pl.pallas_call(back_kernel, out_shape=(jax.ShapeDtypeStruct((32, 4096), F...  8.41 us
  transfers between devices with their start and end apart: 5, of which 4 were waited for; matrix products, arithmetic and copies ran while one was open for 2% of the time, Pallas kernels for 0%

profile of v3, /device:TPU:8, one launch (start us, length us, event | category | flops | bytes accessed | tf_op | source)
XLA Modules:
  0.0 110.4 jit_solution(1855847422135190165)
XLA Ops:
  0.6 8.5 %send_rows.1 = (f32[320,128]{1,0:T(8,128)}, f32[2048,128]{1,0:T(8,128)}) custom-call(f32[16,16]{1,0:T(8,128)} %camera_ref.3, s32[1,64]{1,0:T(1,128)} %chosen_ref.3, s32[64,64]{1,0:T(8,128)} %bitcast.19, f32[59,4096]{1,0:T(8,128)} %params_ref.1), custom_call_target="tpu_custom_call" | custom-call | tf_op jit(solution)/shard_map/send_rows/pallas_call | solution.py:533
  9.1 0.0 copy-start.5
  9.1 12.3 %all-to-all-start = ((f32[64,1,640]{2,1,0:T(1,128)}), f32[64,1,640]{2,1,0:T(1,128)S(1)}, u32[]{:S(2)}, u32[]{:S(2)}) async-start(f32[64,1,640]{2,1,0:T(1,128)} %bitcast.17), calls=%async_computation | async-start | bytes 327680 | tf_op jit(solution)/shard_map/all_to_all | solution.py:587
  21.4 0.0 copy-done.5
  21.4 0.1 copy.18
  21.5 0.8 reshape.29.slots_ref
  22.3 8.8 %all-to-all-done = f32[64,1,640]{2,1,0:T(1,128)S(1)} async-done(((f32[64,1,640]{2,1,0:T(1,128)}), f32[64,1,640]{2,1,0:T(1,128)S(1)}, u32[]{:S(2)}, u32[]{:S(2)}) %all-to-all-start) | async-done | bytes 163872 | tf_op jit(solution)/shard_map/all_to_all | solution.py:587
  31.1 0.0 copy-start.3
  31.1 0.7 copy-done.3
  31.8 20.5 %render.1 = (f32[3,32,256]{2,1,0:T(8,128)}, f32[320,128]{1,0:T(8,128)}) custom-call(s32[1,32]{1,0:T(1,128)} %bitcast.23, f32[320,128]{1,0:T(8,128)} %bitcast.16, s32[2,1,4096]{2,1,0:T(1,128)} %reshape.29.slots_ref, f32[3,32,256]{2,1,0:T(8,128)} %bitcast.21), custom_call_target="tpu_custom_call" | custom-call | tf_op jit(solution)/shard_map/render/pallas_call | solution.py:374
  52.3 16.0 %all_to_all.10 = f32[64,1,640]{2,1,0:T(1,128)} all-to-all(f32[64,1,640]{2,1,0:T(1,128)} %bitcast.18), channel_id=1, replica_groups=mesh['img'=4,'gs'=64] {'gs'}, dimensions={0} | all-to-all | bytes 327680 | tf_op jit(solution)/shard_map/all_to_all | solution.py:591
  68.3 8.4 %pull_rows.1 = (f32[32,4096]{1,0:T(8,128)}, f32[32,4096]{1,0:T(8,128)}) custom-call(f32[16,16]{1,0:T(8,128)} %camera_ref.3, s32[1,64]{1,0:T(1,128)} %chosen_ref.3, s32[64,64]{1,0:T(8,128)} %bitcast.20, f32[2048,128]{1,0:T(8,128)} %get-tuple-element.10.raw_ref, f32[320,128]{1,0:T(8,128)} %bitcast.15), custom_call_target="tpu_custom_call" | custom-call | tf_op jit(solution)/shard_map/pull_rows/pallas_call | solution.py:552
  76.8 1.5 %collective-permute-start = (f32[32,4096]{1,0:T(8,128)}, f32[32,4096]{1,0:T(8,128)S(1)}, u32[]{:S(2)}, u32[]{:S(2)}) collective-permute-start(f32[32,4096]{1,0:T(8,128)} %get-tuple-element.13), channel_id=1, source_target_pairs={{0,64},{64,0},{128,192},{192,128},{1,65},{65,1},{129,193},{193,129... | collective-permute-start | bytes 1572872 | tf_op jit(solution)/shard_map/ppermute | solution.py:605
  78.3 0.0 copy-start.4
  78.3 2.1 %collective-permute-start.2 = (f32[32,4096]{1,0:T(8,128)}, f32[32,4096]{1,0:T(8,128)S(1)}, u32[]{:S(2)}, u32[]{:S(2)}) collective-permute-start(f32[32,4096]{1,0:T(8,128)} %get-tuple-element.14), channel_id=1, source_target_pairs={{0,192},{64,128},{128,64},{192,0},{1,193},{65,129},{129,65},{193,1... | collective-permute-start | bytes 1572872 | tf_op jit(solution)/shard_map/ppermute | solution.py:606
  80.4 10.6 %collective-permute-done = f32[32,4096]{1,0:T(8,128)S(1)} collective-permute-done((f32[32,4096]{1,0:T(8,128)}, f32[32,4096]{1,0:T(8,128)S(1)}, u32[]{:S(2)}, u32[]{:S(2)}) %collective-permute-start) | collective-permute-done | bytes 524320 | tf_op jit(solution)/shard_map/ppermute | solution.py:605
  90.9 1.1 %add.24 = f32[32,4096]{1,0:T(8,128)S(1)} add(f32[32,4096]{1,0:T(8,128)} %get-tuple-element.13, f32[32,4096]{1,0:T(8,128)S(1)} %collective-permute-done) | non-fusion elementwise | flops 131072 | bytes 1572864 | tf_op jit(solution)/shard_map/add | solution.py:605
  92.0 2.8 %collective-permute-start.1 = (f32[32,4096]{1,0:T(8,128)S(1)}, f32[32,4096]{1,0:T(8,128)S(1)}, u32[]{:S(2)}, u32[]{:S(2)}) collective-permute-start(f32[32,4096]{1,0:T(8,128)S(1)} %add.24), channel_id=1, source_target_pairs={{0,192},{64,128},{128,64},{192,0},{1,193},{65,129},{129,65},{193,1... | collective-permute-start | bytes 1572872 | tf_op jit(solution)/shard_map/ppermute | solution.py:608
  94.9 0.0 collective-permute-done.2
  94.9 0.0 copy-done.4
  94.9 0.0 copy-start.6
  94.9 0.1 add.26
  94.9 0.3 collective-permute-start.3
  95.3 11.2 %collective-permute-done.1 = f32[32,4096]{1,0:T(8,128)S(1)} collective-permute-done((f32[32,4096]{1,0:T(8,128)S(1)}, f32[32,4096]{1,0:T(8,128)S(1)}, u32[]{:S(2)}, u32[]{:S(2)}) %collective-permute-start.1) | collective-permute-done | bytes 524320 | tf_op jit(solution)/shard_map/ppermute | solution.py:608
  106.5 0.0 copy-start.1
  106.5 0.0 copy-start.2
  106.5 0.1 add.25
  106.5 0.0 copy-start
  106.5 1.3 %collective-permute-done.3 = f32[32,4096]{1,0:T(8,128)S(1)} collective-permute-done((f32[32,4096]{1,0:T(8,128)S(1)}, f32[32,4096]{1,0:T(8,128)S(1)}, u32[]{:S(2)}, u32[]{:S(2)}) %collective-permute-start.3) | collective-permute-done | bytes 524320 | tf_op jit(solution)/shard_map/ppermute | solution.py:608
  107.9 0.1 add.27
  107.9 0.0 copy-done.6
  107.9 0.0 copy-done.1
  107.9 0.0 copy-done.2
  108.0 0.3 copy-done
  108.3 2.1 %divide_subtract_fusion = (f32[59,4096]{1,0:T(8,128)}, f32[59,4096]{1,0:T(8,128)}, f32[59,4096]{1,0:T(8,128)}) fusion(f32[59,4096]{1,0:T(8,128)S(1)} %copy-done, f32[59]{0:T(128)S(1)} %copy-done.6, f32[32,4096]{1,0:T(8,128)S(1)} %add.27, f32[32,4096]{1,0:T(8,128)S(1)} %add.25, f32[59,4096]{1,0:T(8,128)S(1)} %copy-done.1, f32[59,4096]{1,0:T(8,128)S(1)} %copy-done.2), kind=kLoop, calls=%fused_computation.3 | loop fusion | flops 3141632 | bytes 6848748 | tf_op jit(solution)/shard_map/sub | solution.py:579
Async XLA Ops:
  9.1 12.3 %copy-start.5 = (s32[1,1,32,256]{3,2,1,0:T(8,128)S(1)}, s32[1,1,32,256]{3,2,1,0:T(8,128)}, u32[]{:S(2)}) copy-start(s32[1,1,32,256]{3,2,1,0:T(8,128)} %param.16) | copy-start | bytes 98308
  9.1 22.0 %all-to-all-start = ((f32[64,1,640]{2,1,0:T(1,128)}), f32[64,1,640]{2,1,0:T(1,128)S(1)}, u32[]{:S(2)}, u32[]{:S(2)}) async-start(f32[64,1,640]{2,1,0:T(1,128)} %bitcast.17), calls=%async_computation | async-start | bytes 327680 | tf_op jit(solution)/shard_map/all_to_all | solution.py:587
  31.1 0.7 copy-start.3
  76.8 14.2 %collective-permute-start = (f32[32,4096]{1,0:T(8,128)}, f32[32,4096]{1,0:T(8,128)S(1)}, u32[]{:S(2)}, u32[]{:S(2)}) collective-permute-start(f32[32,4096]{1,0:T(8,128)} %get-tuple-element.13), channel_id=1, source_target_pairs={{0,64},{64,0},{128,192},{192,128},{1,65},{65,1},{129,193},{193,129... | collective-permute-start | bytes 1572872 | tf_op jit(solution)/shard_map/ppermute | solution.py:605
  78.3 16.6 %copy-start.4 = (f32[32,4096]{1,0:T(8,128)S(1)}, f32[32,4096]{1,0:T(8,128)}, u32[]{:S(2)}) copy-start(f32[32,4096]{1,0:T(8,128)} %get-tuple-element.14) | copy-start | bytes 1572868
  78.3 16.6 %collective-permute-start.2 = (f32[32,4096]{1,0:T(8,128)}, f32[32,4096]{1,0:T(8,128)S(1)}, u32[]{:S(2)}, u32[]{:S(2)}) collective-permute-start(f32[32,4096]{1,0:T(8,128)} %get-tuple-element.14), channel_id=1, source_target_pairs={{0,192},{64,128},{128,64},{192,0},{1,193},{65,129},{129,65},{193,1... | collective-permute-start | bytes 1572872 | tf_op jit(solution)/shard_map/ppermute | solution.py:606
  92.0 14.4 %collective-permute-start.1 = (f32[32,4096]{1,0:T(8,128)S(1)}, f32[32,4096]{1,0:T(8,128)S(1)}, u32[]{:S(2)}, u32[]{:S(2)}) collective-permute-start(f32[32,4096]{1,0:T(8,128)S(1)} %add.24), channel_id=1, source_target_pairs={{0,192},{64,128},{128,64},{192,0},{1,193},{65,129},{129,65},{193,1... | collective-permute-start | bytes 1572872 | tf_op jit(solution)/shard_map/ppermute | solution.py:608
  94.9 13.0 %copy-start.6 = (f32[59]{0:T(128)S(1)}, f32[59]{0:T(128)}, u32[]{:S(2)}) copy-start(f32[59]{0:T(128)} %constant.24) | copy-start | bytes 712
  94.9 12.9 %collective-permute-start.3 = (f32[32,4096]{1,0:T(8,128)S(1)}, f32[32,4096]{1,0:T(8,128)S(1)}, u32[]{:S(2)}, u32[]{:S(2)}) collective-permute-start(f32[32,4096]{1,0:T(8,128)S(1)} %add.26), channel_id=1, source_target_pairs={{0,64},{64,0},{128,192},{192,128},{1,65},{65,1},{129,193},{193,129... | collective-permute-start | bytes 1572872 | tf_op jit(solution)/shard_map/ppermute | solution.py:608
  106.5 1.5 %copy-start.1 = (f32[59,4096]{1,0:T(8,128)S(1)}, f32[59,4096]{1,0:T(8,128)}, u32[]{:S(2)}) copy-start(f32[59,4096]{1,0:T(8,128)} %param.11) | copy-start | bytes 2899972
  106.5 1.5 %copy-start.2 = (f32[59,4096]{1,0:T(8,128)S(1)}, f32[59,4096]{1,0:T(8,128)}, u32[]{:S(2)}) copy-start(f32[59,4096]{1,0:T(8,128)} %param.12) | copy-start | bytes 2899972
  106.5 1.8 %copy-start = (f32[59,4096]{1,0:T(8,128)S(1)}, f32[59,4096]{1,0:T(8,128)}, u32[]{:S(2)}) copy-start(f32[59,4096]{1,0:T(8,128)} %params_ref.1) | copy-start | bytes 2899972
